TPU v7x, 128 devices: a whole 4x4x4 slice. The times are simulated.
128 devices in a mesh: row: 4 (over x_lo, core), col: 4 (over z), chan: 8 (over y, x_hi).
Axes of the slice: x: 4 (x_hi: 2, x_lo: 2; x = x_hi * 2 + x_lo), y: 4, z: 4, core: 2. Of those that a mesh axis runs over, the one named last changes fastest.
Arguments:
- visibilities: bfloat16 [64, 1, 4, 2, 512, 512], P('chan', None, None, None, 'row', 'col'), may hold values from -6 to 6
- model: bfloat16 [8, 64, 1, 4, 2, 512, 512], P(None, 'chan', None, None, None, 'row', 'col'), may hold values from -6 to 6
- flags: int32 [64, 512, 512], P('chan', 'row', 'col'), may hold values 0 or 1
- gains: float32 [8, 2, 2, 64, 512], P(None, None, None, 'chan'), may hold values from -3 to 3
- kernel: float32 [5], replicated, may hold values from 0.2 to 1
Outputs:
- gains_out: float32 [8, 2, 2, 64, 512], P(None, None, None, 'chan')
- residual: bfloat16 [64, 1, 4, 2, 512, 512], P('chan', None, None, None, 'row', 'col')
All inputs are finite; a program needn't handle non-finite values. No bound on the sum of `flags` on one device may be relied on, other than what follows from the above.
Results may differ from a plain program's by a relative error of at most 0.001.
Values sent between devices are 32-bit elements; how exact they have to be, the bound alone decides.
No kernel may reach another device: no remote copies, remote signals or barrier semaphores. Data moves between devices by JAX's collectives and lax.ppermute only.
A program may use at most 192 MiB of HBM per device.

v0:
```python
import jax
import jax.numpy as jnp
import numpy as np
from jax import lax
from jax.sharding import PartitionSpec as P

ITERS = 3


A_POL = np.array([0, 0, 1, 1])
B_POL = np.array([0, 1, 0, 1])
LAMBDA = 1.0


def padded_2(block, sides, width):
    for axis, dim in sides:
        count = lax.axis_size(axis)
        forward = [(i, i + 1) for i in range(count - 1)]
        backward = [(target, source) for source, target in forward]
        low = lax.ppermute(
            lax.slice_in_dim(block, block.shape[dim] - width, None, axis=dim), axis, forward
        )
        high = lax.ppermute(lax.slice_in_dim(block, 0, width, axis=dim), axis, backward)
        block = jnp.concatenate([low, block, high], axis=dim)
    return block


def block_terms(vis_c, model_c, weight, gain_rows, gain_cols):
    count = gain_rows.shape[0]
    rows = gain_rows.shape[3]
    cols = gain_cols.shape[3]
    rows_re = gain_rows[:, 0][:, A_POL][:, None, :, :, None]
    rows_im = gain_rows[:, 1][:, A_POL][:, None, :, :, None]
    cols_re = gain_cols[:, 0][:, B_POL][:, None, :, None, :]
    cols_im = gain_cols[:, 1][:, B_POL][:, None, :, None, :]
    model_re = model_c[:, :, :, 0].astype(jnp.float32)
    model_im = model_c[:, :, :, 1].astype(jnp.float32)
    along_re = model_re * cols_re + model_im * cols_im
    along_im = model_im * cols_re - model_re * cols_im
    guess_re = rows_re * along_re - rows_im * along_im
    guess_im = rows_re * along_im + rows_im * along_re
    mask = weight[None, None, None]
    resid_re = vis_c[:, :, 0].astype(jnp.float32) - jnp.sum(guess_re, axis=0)
    resid_im = vis_c[:, :, 1].astype(jnp.float32) - jnp.sum(guess_im, axis=0)
    peeled_re = resid_re[None] + guess_re
    peeled_im = resid_im[None] + guess_im
    paired_re = rows_re * model_re - rows_im * model_im
    paired_im = rows_re * model_im + rows_im * model_re
    row_top_re = jnp.sum(mask * (peeled_re * along_re + peeled_im * along_im), axis=(1, 4))
    row_top_im = jnp.sum(mask * (peeled_im * along_re - peeled_re * along_im), axis=(1, 4))
    row_bottom = jnp.sum(mask * (along_re * along_re + along_im * along_im), axis=(1, 4))
    col_top_re = jnp.sum(mask * (peeled_re * paired_re + peeled_im * paired_im), axis=(1, 3))
    col_top_im = jnp.sum(mask * (peeled_re * paired_im - peeled_im * paired_re), axis=(1, 3))
    col_bottom = jnp.sum(mask * (paired_re * paired_re + paired_im * paired_im), axis=(1, 3))
    row_numer = jnp.stack([row_top_re, row_top_im], 1).reshape(count, 2, 2, 2, rows).sum(3)
    row_denom = row_bottom.reshape(count, 2, 2, rows).sum(2)
    col_numer = jnp.stack([col_top_re, col_top_im], 1).reshape(count, 2, 2, 2, cols).sum(2)
    col_denom = col_bottom.reshape(count, 2, 2, cols).sum(1)
    residual = (jnp.stack([resid_re, resid_im], 2) * weight).astype(jnp.bfloat16)
    return (row_numer, row_denom, col_numer, col_denom, residual)


def renew(gains_now, numer, denom):
    solved = numer / (denom[:, None] + LAMBDA)
    return 0.5 * (gains_now + solved)


def blend(padded, kernel, channels, first, total_channels):
    span = kernel.shape[0]
    reach = span // 2
    index = first + jnp.arange(channels, dtype=jnp.int32)
    shape = padded.shape[:3] + (channels,) + padded.shape[4:]
    total = jnp.zeros(shape, jnp.float32)
    coverage = jnp.zeros((channels,), jnp.float32)
    for offset in range(span):
        total = total + kernel[offset] * padded[:, :, :, offset : offset + channels]
        source = index + offset - reach
        inside = ((source >= 0) & (source < total_channels)).astype(jnp.float32)
        coverage = coverage + kernel[offset] * inside
    return total / coverage[:, None]


def local(visibilities, model, flags, gains, kernel):
    channels = visibilities.shape[0]
    rows = visibilities.shape[4]
    cols = visibilities.shape[5]
    stations = gains.shape[4]
    reach = kernel.shape[0] // 2
    row_start = lax.axis_index("row") * rows
    col_start = lax.axis_index("col") * cols
    first = lax.axis_index("chan") * channels
    total_channels = channels * lax.axis_size("chan")

    def local_terms(gains_now, channel):
        vis_c = lax.dynamic_index_in_dim(visibilities, channel, 0, keepdims=False)
        model_c = lax.dynamic_index_in_dim(model, channel, 1, keepdims=False)
        weight = lax.dynamic_index_in_dim(flags, channel, 0, keepdims=False).astype(jnp.float32)
        gain_c = lax.dynamic_index_in_dim(gains_now, channel, 3, keepdims=False)
        gain_rows = lax.dynamic_slice_in_dim(gain_c, row_start, rows, 3)
        gain_cols = lax.dynamic_slice_in_dim(gain_c, col_start, cols, 3)
        return block_terms(vis_c, model_c, weight, gain_rows, gain_cols)

    for sweep in range(ITERS):
        sums_gains_now = gains

        def one(channel):
            row_numer, row_denom, col_numer, col_denom, _ = local_terms(sums_gains_now, channel)
            numer_zero = jnp.zeros(row_numer.shape[:3] + (stations,), jnp.float32)
            denom_zero = jnp.zeros(row_denom.shape[:2] + (stations,), jnp.float32)
            numer = lax.dynamic_update_slice_in_dim(numer_zero, row_numer, row_start, 3)
            numer = numer + lax.dynamic_update_slice_in_dim(numer_zero, col_numer, col_start, 3)
            denom = lax.dynamic_update_slice_in_dim(denom_zero, row_denom, row_start, 2)
            denom = denom + lax.dynamic_update_slice_in_dim(denom_zero, col_denom, col_start, 2)
            return (numer, denom)

        numer, denom = lax.map(one, jnp.arange(channels, dtype=jnp.int32))
        numer, denom = (jnp.moveaxis(numer, 0, 3), jnp.moveaxis(denom, 0, 2))
        numer, denom = lax.psum((numer, denom), ("row", "col"))
        averaged = renew(gains, numer, denom)
        padded = padded_2(averaged, (("chan", 3),), reach)
        gains = blend(padded, kernel, channels, first, total_channels)

    def final(channel):
        return local_terms(gains, channel)[4]

    residual = lax.map(final, jnp.arange(channels, dtype=jnp.int32))
    return (gains, residual)


def solution(mesh):
    placed = (
        P("chan", None, None, None, "row", "col"),
        P(None, "chan", None, None, None, "row", "col"),
        P("chan", "row", "col"),
        P(None, None, None, "chan", None),
        P(),
    )
    return jax.shard_map(
        local,
        mesh=mesh,
        in_specs=placed,
        out_specs=(P(None, None, None, "chan", None), P("chan", None, None, None, "row", "col")),
        check_vma=False,
    )
```

profile of v0, /device:TPU:25, one launch (start us, length us, event | category | flops | bytes accessed | tf_op | source)
XLA Modules:
  0.0 1006.7 jit_solution(4179838460937187098)
XLA Ops:
  7.2 14.3 %copy.156 = bf16[8,8,1,4,2,128,128]{6,5,4,3,0,2,1:T(8,128)(2,1)} copy(bf16[8,8,1,4,2,128,128]{6,5,4,3,2,1,0:T(8,128)(2,1)} %param.32) | data formatting | bytes 33554432
  24.3 152.7 %while.66 = (s32[]{:T(128)}, f32[8,8,2,2,512]{4,0,3,2,1:T(8,128)S(1)}, f32[8,8,2,512]{3,1,2,0:T(8,128)S(1)}, s32[8]{0:T(128)}, s32[8,128,128]{2,1,0:T(8,128)}, /...) while((s32[]{:T(128)}, ...), condition=%wide.region_13.14_spmd.clone.clone, body=%wide.region_0.13_spmd.sunk.clone.clone.sunk | while | flops 35811332 | bytes 13123979 | solution.py:116
  32.1 1.7 dynamic-slice_bitcast_fusion.29
  36.2 5.0 multiply_reduce_fusion.21
  51.2 1.7 dynamic-slice_bitcast_fusion.29
  55.3 5.0 multiply_reduce_fusion.21
  70.3 1.7 dynamic-slice_bitcast_fusion.29
  74.4 5.0 multiply_reduce_fusion.21
  89.4 1.7 dynamic-slice_bitcast_fusion.29
  93.5 5.0 multiply_reduce_fusion.21
  108.5 1.7 dynamic-slice_bitcast_fusion.29
  112.6 5.0 multiply_reduce_fusion.21
  127.6 1.7 dynamic-slice_bitcast_fusion.29
  131.7 5.0 multiply_reduce_fusion.21
  146.7 1.7 dynamic-slice_bitcast_fusion.29
  150.8 5.0 multiply_reduce_fusion.21
  165.7 1.7 dynamic-slice_bitcast_fusion.29
  169.9 5.0 multiply_reduce_fusion.21
  178.0 122.3 %all-reduce.11.cloned.1.call-done = (f32[8,2,2,8,512]{4,3,2,1,0:T(8,128)}, f32[8,2,8,512]{3,0,1,2:T(8,128)}) async-done(((f32[8,2,2,8,512]{4,3,2,1,0:T(8,128)}, f32[8,2,8,512]{3,0,1,2:T(8,128)}), (f32[8,2,2,8,512]{4,3,2,1,0:T(8,128)}, f32[8,2,8,512]{3,0,1,2:T(8,128)})) %all-reduce.11.cloned.1.call-update) | async-done | bytes 786448 | tf_op jit(solution)/shard_map/psum | solution.py:118
  303.5 4.3 collective-permute-start
  307.9 3.4 collective-permute-start.1
  312.5 3.1 fusion.66
  315.7 5.2 fusion.52
  322.9 151.0 %while.67 = (s32[]{:T(128)}, f32[8,8,2,2,512]{4,0,3,2,1:T(8,128)}, f32[8,8,2,512]{3,1,2,0:T(8,128)S(1)}, s32[8]{0:T(128)S(1)}, s32[8,128,128]{2,1,0:T(8,128)}, /...) while((s32[]{:T(128)}, f32[8,8,2,2,512]{4,0,3,2,1:T(8,128)}, ...), condition=%wide.region_29.30_spmd.clone.clone, body=%wide.region_16.29_spmd.sunk.clone.clone.sunk | while | flops 35811332 | bytes 13123979 | solution.py:116
  330.2 1.7 dynamic-slice_bitcast_fusion.32
  334.4 5.0 multiply_reduce_fusion.22
  339.7 2.1 dynamic_update_slice.273
  349.1 1.7 dynamic-slice_bitcast_fusion.32
  353.3 5.0 multiply_reduce_fusion.22
  358.6 2.1 dynamic_update_slice.273
  372.1 5.0 multiply_reduce_fusion.22
  377.5 2.1 dynamic_update_slice.273
  391.0 5.0 multiply_reduce_fusion.22
  396.4 2.1 dynamic_update_slice.273
  409.9 5.0 multiply_reduce_fusion.22
  415.2 2.1 dynamic_update_slice.273
  428.8 5.0 multiply_reduce_fusion.22
  434.1 2.1 dynamic_update_slice.273
  443.5 1.7 dynamic-slice_bitcast_fusion.32
  447.6 5.0 multiply_reduce_fusion.22
  453.0 2.1 dynamic_update_slice.273
  466.5 5.0 multiply_reduce_fusion.22
  471.8 2.1 dynamic_update_slice.273
  474.7 121.4 %all-reduce.9.cloned.1.call-done = (f32[8,2,2,8,512]{4,3,2,1,0:T(8,128)}, f32[8,2,8,512]{3,0,1,2:T(8,128)}) async-done(((f32[8,2,2,8,512]{4,3,2,1,0:T(8,128)}, f32[8,2,8,512]{3,0,1,2:T(8,128)}), (f32[8,2,2,8,512]{4,3,2,1,0:T(8,128)}, f32[8,2,8,512]{3,0,1,2:T(8,128)})) %all-reduce.9.cloned.1.call-update) | async-done | bytes 786448 | tf_op jit(solution)/shard_map/psum | solution.py:118
  599.3 4.3 collective-permute-start.2
  603.6 3.5 collective-permute-start.3
  607.9 3.0 collective-permute-done.3
  610.9 5.1 fusion.43
  617.8 152.1 %while.68 = (s32[]{:T(128)}, f32[8,8,2,2,512]{4,0,3,2,1:T(8,128)S(1)}, f32[8,8,2,512]{3,1,2,0:T(8,128)S(1)}, s32[8]{0:T(128)}, s32[8,128,128]{2,1,0:T(8,128)}, /...) while((s32[]{:T(128)}, ...), condition=%wide.region_45.46_spmd.clone.clone, body=%wide.region_32.45_spmd.sunk.clone.clone.sunk | while | flops 35811332 | bytes 13123979 | solution.py:116
  629.6 5.0 multiply_reduce_fusion.23
  648.6 5.0 multiply_reduce_fusion.23
  663.5 1.7 dynamic-slice_bitcast_fusion.35
  667.6 5.0 multiply_reduce_fusion.23
  686.7 5.0 multiply_reduce_fusion.23
  705.7 5.0 multiply_reduce_fusion.23
  724.7 5.0 multiply_reduce_fusion.23
  743.7 5.0 multiply_reduce_fusion.23
  762.7 5.0 multiply_reduce_fusion.23
  770.8 122.1 %all-reduce.7.cloned.1.call-done = (f32[8,2,2,8,512]{4,3,2,1,0:T(8,128)}, f32[8,2,8,512]{3,0,1,2:T(8,128)}) async-done(((f32[8,2,2,8,512]{4,3,2,1,0:T(8,128)}, f32[8,2,8,512]{3,0,1,2:T(8,128)}), (f32[8,2,2,8,512]{4,3,2,1,0:T(8,128)}, f32[8,2,8,512]{3,0,1,2:T(8,128)})) %all-reduce.7.cloned.1.call-update) | async-done | bytes 786448 | tf_op jit(solution)/shard_map/psum | solution.py:118
  896.0 4.3 collective-permute-start.4
  900.3 3.4 collective-permute-start.5
  904.8 3.0 collective-permute-done.5
  907.8 4.2 fusion.34
  913.2 87.0 %while.69 = (s32[]{:T(128)}, bf16[8,1,4,2,128,128]{5,4,3,2,1,0:T(8,128)(2,1)}, s32[8]{0:T(128)S(1)}, bf16[8,1,4,2,128,128]{5,4,2,3,1,0:T(8,128)(2,1)S(1)}, f32[8...) while((s32[]{:T(128)}, ...), condition=%wide.region_51.52_spmd.clone.clone, body=%wide.region_48.51_spmd.sunk.clone.clone.sunk | while | flops 8931334 | bytes 10101571 | solution.py:126
  (1085 shorter events, 339.9 us)
Async XLA Ops:
  7.2 293.2 %all-reduce.11.cloned.1.call-start = ((), (), s32[]{:S(2)}) async-start(), calls=%async_computation.2 | async-start | bytes 1572864 | tf_op jit(solution)/shard_map/psum | solution.py:118
  7.2 14.3 %copy-start.5 = (bf16[8,1,4,2,128,128]{5,4,3,2,1,0:T(8,128)(2,1)S(1)}, bf16[8,1,4,2,128,128]{5,4,3,2,1,0:T(8,128)(2,1)}, u32[]{:S(2)}) copy-start(bf16[8,1,4,2,128,128]{5,4,3,2,1,0:T(8,128)(2,1)} %param.31) | copy-start | bytes 6291460
  21.5 1.0 copy-start
  177.1 0.8 copy-start.3
  177.1 0.9 copy-start.7
  178.0 133.2 %copy-start.10 = (f32[5]{0:T(128)S(1)}, f32[5]{0:T(128)}, u32[]{:S(2)}) copy-start(f32[5]{0:T(128)} %param.35) | copy-start | bytes 64
  178.0 418.1 %all-reduce.9.cloned.1.call-start = ((), (), s32[]{:S(2)}) async-start(), calls=%async_computation.1 | async-start | bytes 1572864 | tf_op jit(solution)/shard_map/psum | solution.py:118
  302.6 0.8 copy-start.1
  303.5 12.2 %collective-permute-start = (f32[8,2,2,2,512]{4,3,2,1,0:T(2,128)S(1)}, f32[8,2,2,2,512]{4,3,2,1,0:T(2,128)S(1)}, u32[]{:S(2)}, u32[]{:S(2)}) collective-permute-start(f32[8,2,2,2,512]{4,3,2,1,0:T(2,128)S(1)} %get-tuple-element.1721), channel_id=1, source_target_pairs={{0,1},{1,2},{2,3},{3,4},{4,5},{5,6},{6,7},{8,9},{9,10},{10,11},{11... | collective-permute-start | bytes 393224 | tf_op jit(solution)/shard_map/ppermute | solution.py:20
  307.9 7.9 collective-permute-start.1
  315.7 295.2 %copy-start.11 = (f32[8]{0:T(128)}, f32[8]{0:T(128)S(1)}, u32[]{:S(2)}) copy-start(f32[8]{0:T(128)S(1)} %fusion.66) | copy-start | bytes 100
  473.9 0.7 copy-start.8
  474.7 418.2 %all-reduce.7.cloned.1.call-start = ((), (), s32[]{:S(2)}) async-start(), calls=%async_computation | async-start | bytes 1572864 | tf_op jit(solution)/shard_map/psum | solution.py:118
  598.4 0.8 copy-start.2
  599.3 8.6 collective-permute-start.2
  603.6 7.3 collective-permute-start.3
  769.9 0.8 copy-start.4
  769.9 0.9 copy-start.9
  770.8 137.0 %copy-start.12 = (f32[8]{0:T(128)S(1)}, f32[8]{0:T(128)}, u32[]{:S(2)}) copy-start(f32[8]{0:T(128)} %copy-done.11) | copy-start | bytes 100
  896.0 8.8 collective-permute-start.4
  900.3 7.5 collective-permute-start.5
  912.1 0.8 copy-start.6
Sparse Core Ops, SparseCore 0:
  178.1 122.1 all-reduce.10
  474.8 121.2 all-reduce.8
  770.9 121.8 all-reduce.6
where the time goes:
time: 1020 us; the launch traced here: 1010 us
  waiting for transfers between devices  374 us (37%)
  other arithmetic  291 us (29%)
  local copies, waits for them, and re-layouts  237 us (23%)
  loops' own time  67.8 us (7%)
  starting transfers between devices  23.3 us (2%)
  between operations  14.7 us (1%)
    psum x3, waiting for transfers between devices, local(): numer, denom = lax.psum((numer, denom), ('row', 'col'))  366 us
    reduce_sum x24, other arithmetic, block_terms(): jnp.sum(mask * (peeled_re * paired_re + peeled_im * paired_im), axis=(1, 3))  120 us
    squeeze x32, local copies, waits for them, and re-layouts, local_terms(): model_c = lax.dynamic_index_in_dim(model, channel, 1, keepdims=False)  55.5 us
    another operation x3, loops' own time, local(): numer, denom = lax.map(one, jnp.arange(channels, dtype=jnp.int32))  53.5 us
    reduce_sum x32, other arithmetic, block_terms(): resid_re = vis_c[:, :, 0].astype(jnp.float32) - jnp.sum(guess_re, axis=0)  46.6 us
    dynamic_slice x32, local copies, waits for them, and re-layouts, local(): numer, denom = lax.map(one, jnp.arange(channels, dtype=jnp.int32))  29.6 us
    dynamic_update_slice x72, local copies, waits for them, and re-layouts, local(): numer, denom = lax.map(one, jnp.arange(channels, dtype=jnp.int32))  27.5 us
    convert_element_type x32, other arithmetic, local_terms(): lax.dynamic_index_in_dim(flags, channel, 0, keepdims=False)  27.3 us
  transfers between devices with their start and end apart: 9, of which 7 were waited for; matrix products, arithmetic and copies ran while one was open for 0% of the time, Pallas kernels for 0%

commit v1 on v0

v1 whole, which is shorter than its diff:
```python
import functools

import jax
import jax.numpy as jnp
import numpy as np
from jax import lax
from jax.experimental import pallas as pl
from jax.experimental.pallas import tpu as pltpu
from jax.sharding import PartitionSpec as P

ITERS = 3
GRID = ("row", "col")
TILE = 16


def spread_matrix(count):
    spread = np.zeros((count, 2, 2, count, 2, TILE), np.float32)
    for k in range(count):
        spread[k, 0, 0, k, 0] = 1.0
        spread[k, 1, 0, k, 1] = -1.0
        spread[k, 1, 1, k, 0] = 1.0
        spread[k, 0, 1, k, 1] = 1.0
    return spread.reshape(2 * count, 4 * count * TILE)


def split(value):
    high = value.astype(jnp.bfloat16)
    low = (value - high.astype(jnp.float32)).astype(jnp.bfloat16)
    return high, low


def kernel(first, final, place, *refs):
    refs = list(refs)
    take = refs.pop
    model, vis, flags, spread = take(0), take(0), take(0), take(0)
    row_parts = [take(0) for _ in range(1 if first else 4)]
    col_parts = [take(0) for _ in range(1 if first else 4)]
    if final:
        resid = take(0)
    else:
        row_out = [take(0) for _ in range(4)]
        col_out = [take(0) for _ in range(4)]
    g_row, g_col, g_mat, w_row, w_col, left, masked, terms = refs
    count = model.shape[0]
    channel = pl.program_id(0)
    me_row, me_col = place[0], place[1]
    f32, bf16 = jnp.float32, jnp.bfloat16

    @pl.when(channel == 0)
    def prepare():
        if first:
            g_row[...] = row_parts[0][...]
            g_col[...] = col_parts[0][...]
        else:
            for m in range(4):
                at = lax.rem(me_col + 4 - m, 4)
                g_row[pl.ds(at * 2, 2)] = row_parts[m][...]
                at = lax.rem(me_row + 4 - m, 4)
                g_col[pl.ds(at * 2, 2)] = col_parts[m][...]
        for k in range(count):
            for pol in range(2):
                lanes = slice(pol * 128, pol * 128 + 128)
                for part in range(2):
                    g_mat[:, 2 * k + part, lanes] = g_row[k, part, pol]
                if not final:
                    for source, weights in ((g_row, w_row), (g_col, w_col)):
                        re, im = source[k, 0, pol], source[k, 1, pol]
                        for n, value in enumerate((re, im, re * re + im * im)):
                            high = value.astype(bf16).astype(f32)
                            weights[:, k, n, lanes] = high
                            weights[:, k, 4 + n, lanes] = value - high
                        zero = jnp.zeros_like(re)
                        for n in (3, 7, 8, 9, 10, 11, 12, 13, 14, 15):
                            weights[:, k, n, lanes] = zero

    gains_c = jnp.transpose(g_mat[channel])
    high, low = split(gains_c)
    width = 2 * count * TILE
    same = (
        lax.broadcasted_iota(jnp.int32, (128, 2 * width), 0) % TILE
        == lax.broadcasted_iota(jnp.int32, (128, 2 * width), 1) % TILE
    )
    for h, value in enumerate((high, low)):
        for pol in range(2):
            wide = jnp.dot(value[pol * 128 : pol * 128 + 128], spread[...], preferred_element_type=f32)
            wide = jnp.where(same, wide, 0.0).astype(bf16)
            for part in range(2):
                left[pol, :, (2 * h + part) * TILE : (2 * h + part + 1) * TILE, :] = wide[
                    :, part * width : (part + 1) * width
                ].reshape(128 // TILE, TILE, width)

    def residual_tile(step, _):
        pol, tile = step // 8, step % 8
        rows = pl.ds(pl.multiple_of(tile * TILE, TILE), TILE)
        stacks = []
        for b in range(2):
            parts, lows = [], []
            for k in range(count):
                m_re = model[k, 0, 0, 2 * pol + b, 0, rows, :].astype(f32)
                m_im = model[k, 0, 0, 2 * pol + b, 1, rows, :].astype(f32)
                q_re = g_col[k, 0, b, pl.ds(channel, 1), :]
                q_im = g_col[k, 1, b, pl.ds(channel, 1), :]
                z_re = m_re * q_re + m_im * q_im
                z_im = m_im * q_re - m_re * q_im
                for z in (z_re, z_im):
                    if final:
                        z_high, z_low = split(z)
                        parts.append(z_high)
                        lows.append(z_low)
                    else:
                        parts.append(z.astype(bf16))
            stacks.append((jnp.concatenate(parts, 0), jnp.concatenate(lows, 0) if final else None))
        gains_t = left[pol, tile]
        guess = jnp.dot(gains_t, jnp.concatenate([s[0] for s in stacks], 1), preferred_element_type=f32)
        if final:
            guess += jnp.dot(gains_t, jnp.concatenate([s[1] for s in stacks], 1), preferred_element_type=f32)
        weight = flags[0, rows, :].astype(f32)
        out_rows = pl.ds(pl.multiple_of(step * TILE, TILE), TILE)
        for b in range(2):
            for part in range(2):
                lanes = slice(b * 128, b * 128 + 128)
                total = (
                    guess[part * TILE : (part + 1) * TILE, lanes]
                    + guess[(2 + part) * TILE : (3 + part) * TILE, lanes]
                )
                seen = vis[0, 0, 2 * pol + b, part, rows, :].astype(f32)
                value = (seen - total) * weight
                if final:
                    resid[0, 0, 2 * pol + b, part, rows, :] = value.astype(bf16)
                else:
                    masked[part, out_rows, lanes] = value
        return 0

    lax.fori_loop(0, 16, residual_tile, 0, unroll=4)
    if final:
        return

    def product_tile(step, _):
        pol, tile = step // 8, step % 8
        rows = pl.ds(pl.multiple_of(tile * TILE, TILE), TILE)
        weight = flags[0, rows, :].astype(f32).astype(bf16)
        out_rows = pl.ds(pl.multiple_of(step * TILE, TILE), TILE)
        for b in range(2):
            lanes = slice(b * 128, b * 128 + 128)
            r_re = masked[0, out_rows, lanes]
            r_im = masked[1, out_rows, lanes]
            for k in range(count):
                m_re = model[k, 0, 0, 2 * pol + b, 0, rows, :]
                m_im = model[k, 0, 0, 2 * pol + b, 1, rows, :]
                terms[k, 4, out_rows, lanes] = (m_re * m_re + m_im * m_im) * weight
                m_re, m_im = m_re.astype(f32), m_im.astype(f32)
                for x, value in enumerate((r_re * m_re + r_im * m_im, r_im * m_re - r_re * m_im)):
                    high, low = split(value)
                    terms[k, 2 * x, out_rows, lanes] = high
                    terms[k, 2 * x + 1, out_rows, lanes] = low
        return 0

    lax.fori_loop(0, 16, product_tile, 0, unroll=2)

    for m in range(4):
        for outs, mine, gains in ((row_out[m], me_col, g_row), (col_out[m], me_row, g_col)):
            for two in range(2):
                k = lax.rem(mine + m, 4) * 2 + two
                is_row = gains is g_row
                if is_row:
                    weights = w_col[channel, k].astype(bf16)
                    sums = [
                        lax.dot_general(weights, terms[k, x], (((1,), (1,)), ((), ())), preferred_element_type=f32)
                        for x in range(5)
                    ]
                else:
                    weights = w_row[channel, k].astype(bf16)
                    sums = [jnp.dot(weights, terms[k, x], preferred_element_type=f32) for x in range(5)]
                sums = [sums[0] + sums[1], sums[2] + sums[3], sums[4]]
                sums = [s[0:4] + s[4:8] for s in sums]
                if is_row:
                    top_re = sums[0][0:1] - sums[1][1:2]
                    top_im = sums[0][1:2] + sums[1][0:1]
                else:
                    top_re = sums[0][0:1] + sums[1][1:2]
                    top_im = sums[0][1:2] - sums[1][0:1]
                below = sums[2][2:3]
                factor = 2.0 * below + 0.25 if is_row else 2.0 * below
                for pol in range(2):
                    lanes = slice(pol * 128, pol * 128 + 128)
                    at = pl.ds(channel, 1)
                    outs[two, 0, pol, at, :] = top_re[:, lanes] + gains[k, 0, pol, at, :] * factor[:, lanes]
                    outs[two, 1, pol, at, :] = top_im[:, lanes] + gains[k, 1, pol, at, :] * factor[:, lanes]
                    outs[two, 2, pol, at, :] = below[:, lanes]


def sweep(first, final, place, model, vis, flags, row_parts, col_parts):
    count, channels = model.shape[0], model.shape[1]
    f32, bf16 = jnp.float32, jnp.bfloat16
    spread = jnp.asarray(spread_matrix(count), bf16)

    def whole(shape):
        return pl.BlockSpec(shape, lambda c, place: (0,) * len(shape))

    in_specs = [
        pl.BlockSpec((count, 1, 1, 4, 2, 128, 128), lambda c, place: (0, c, 0, 0, 0, 0, 0)),
        pl.BlockSpec((1, 1, 4, 2, 128, 128), lambda c, place: (c, 0, 0, 0, 0, 0)),
        pl.BlockSpec((1, 128, 128), lambda c, place: (c, 0, 0)),
        whole(spread.shape),
    ]
    if first:
        block = (count, 2, 2, channels, 128)
        in_specs += [
            pl.BlockSpec(block, lambda c, place: (0, 0, 0, 0, place[0])),
            pl.BlockSpec(block, lambda c, place: (0, 0, 0, 0, place[1])),
        ]
    else:
        in_specs += [whole(part.shape) for part in (*row_parts, *col_parts)]
    if final:
        out_shape = jax.ShapeDtypeStruct(vis.shape, bf16)
        out_specs = pl.BlockSpec((1, 1, 4, 2, 128, 128), lambda c, place: (c, 0, 0, 0, 0, 0))
    else:
        shape = (count // 4, 3, 2, channels, 128)
        out_shape = [jax.ShapeDtypeStruct(shape, f32)] * 8
        out_specs = [whole(shape)] * 8
    return pl.pallas_call(
        functools.partial(kernel, first, final),
        out_shape=out_shape,
        grid_spec=pltpu.PrefetchScalarGridSpec(
            num_scalar_prefetch=1,
            grid=(channels,),
            in_specs=in_specs,
            out_specs=out_specs,
            scratch_shapes=[
                pltpu.VMEM((count, 2, 2, channels, 128), f32),
                pltpu.VMEM((count, 2, 2, channels, 128), f32),
                pltpu.VMEM((channels, 2 * count, 256), f32),
                pltpu.VMEM((channels, count, 16, 256), f32),
                pltpu.VMEM((channels, count, 16, 256), f32),
                pltpu.VMEM((2, 8, 4 * TILE, 2 * count * TILE), bf16),
                pltpu.VMEM((2, 256, 256), f32),
                pltpu.VMEM((count, 5, 256, 256), bf16),
            ],
        ),
        compiler_params=pltpu.CompilerParams(vmem_limit_bytes=48 * 1024 * 1024),
        cost_estimate=pl.CostEstimate(flops=10**10, bytes_accessed=20 * 10**6, transcendentals=0),
    )(place, model, vis, flags, spread, *row_parts, *col_parts)


def move(block, target):
    pairs = []
    for row in range(4):
        for col in range(4):
            to_row, to_col = target(row, col)
            pairs.append((row * 4 + col, to_row * 4 + to_col))
    return lax.ppermute(block, GRID, pairs)


def smooth(averaged, kernel_weights, first, total_channels):
    span = kernel_weights.shape[0]
    reach = span // 2
    channels = averaged.shape[3]
    chans = lax.axis_size("chan")
    forward = [(i, i + 1) for i in range(chans - 1)]
    backward = [(i + 1, i) for i in range(chans - 1)]
    low = lax.ppermute(averaged[:, :, :, channels - reach :], "chan", forward)
    high = lax.ppermute(averaged[:, :, :, :reach], "chan", backward)
    padded = jnp.concatenate([low, averaged, high], axis=3)
    index = first + jnp.arange(channels, dtype=jnp.int32)
    total = jnp.zeros(averaged.shape, jnp.float32)
    coverage = jnp.zeros((channels,), jnp.float32)
    for offset in range(span):
        total = total + kernel_weights[offset] * padded[:, :, :, offset : offset + channels]
        source = index + offset - reach
        inside = ((source >= 0) & (source < total_channels)).astype(jnp.float32)
        coverage = coverage + kernel_weights[offset] * inside
    return total / coverage[:, None]


def in_order(parts, mine):
    chunks = []
    for chunk in range(4):
        value = parts[0]
        for m in range(1, 4):
            value = jnp.where(lax.rem(mine + 4 - m, 4) == chunk, parts[m], value)
        chunks.append(value)
    return jnp.concatenate(chunks, 0)


def local(visibilities, model, flags, gains, kernel_weights):
    channels = visibilities.shape[0]
    me_row, me_col = lax.axis_index("row"), lax.axis_index("col")
    place = jnp.stack([me_row, me_col]).astype(jnp.int32)
    first = lax.axis_index("chan") * channels
    total_channels = channels * lax.axis_size("chan")
    row_parts, col_parts = [gains], [gains]
    for step in range(ITERS):
        outs = sweep(step == 0, False, place, model, visibilities, flags, row_parts, col_parts)
        total = outs[0]
        for m in range(1, 4):
            total = total + move(outs[m], lambda i, j, m=m: (i, (j + m) % 4))
        for m in range(4):
            total = total + move(outs[4 + m], lambda i, j, m=m: (j, (i + m) % 4))
        averaged = 0.5 * total[:, :2] / (total[:, 2:] + 1.0)
        mine = smooth(averaged, kernel_weights, first, total_channels)
        row_parts = [mine] + [move(mine, lambda i, j, m=m: (i, (j + m) % 4)) for m in range(1, 4)]
        col_parts = [move(mine, lambda i, j, m=m: ((j + m) % 4, i)) for m in range(4)]
    block = in_order(row_parts, me_col)
    blocks = [block] + [move(block, lambda i, j, m=m: ((i + m) % 4, j)) for m in range(1, 4)]
    residual = sweep(False, True, place, model, visibilities, flags, row_parts, col_parts)
    columns = []
    for chunk in range(4):
        value = blocks[0]
        for m in range(1, 4):
            value = jnp.where(lax.rem(me_row + 4 - m, 4) == chunk, blocks[m], value)
        columns.append(value)
    return jnp.concatenate(columns, 4), residual


def solution(mesh):
    placed = (
        P("chan", None, None, None, "row", "col"),
        P(None, "chan", None, None, None, "row", "col"),
        P("chan", "row", "col"),
        P(None, None, None, "chan", None),
        P(),
    )
    return jax.shard_map(
        local,
        mesh=mesh,
        in_specs=placed,
        out_specs=(P(None, None, None, "chan", None), P("chan", None, None, None, "row", "col")),
        check_vma=False,
    )
```

time: 1020 us -> 314 us (0.31)
  waiting for transfers between devices: 374 us -> 25.3 us
  other arithmetic: 291 us -> 14.1 us
  local copies, waits for them, and re-layouts: 237 us -> 5.08 us
  Pallas kernels: 0 us -> 164 us
  starting transfers between devices: 23.3 us -> 99.7 us
  loops' own time: 67.8 us -> 0 us
  between operations: 14.7 us -> 1 us
    psum x3 -> x0, waiting for transfers between devices: 366 us -> none  [local(): numer, denom = lax.psum((numer, denom), ('row', 'col'))]
    reduce_sum x152 -> x0, other arithmetic: 177 us -> none  [the longest x24 120 us: block_terms(): jnp.sum(mask * (peeled_re * paired_re + peeled_im * paired_im), axis=(1, 3))]
    pallas_call x0 -> x4, Pallas kernels: none -> 164 us  [sweep(): pl.pallas_call(functools.partial(kernel, first, final), out_shape=out_sha...]
    ppermute x6 -> x51, starting transfers between devices: 23.2 us -> 99.7 us  [the longest x45 76.6 us: move(): return lax.ppermute(block, GRID, pairs)]
    gather x256 -> x0, local copies, waits for them, and re-layouts: 71.1 us -> none  [the longest x64 17.8 us: block_terms(): cols_re = gain_cols[:, 0][:, B_POL][:, None, :, None, :]]
    another operation x4 -> x0, loops' own time: 67.8 us -> none  [the longest x3 53.5 us: local(): numer, denom = lax.map(one, jnp.arange(channels, dtype=jnp.int32))]
    squeeze x96 -> x0, local copies, waits for them, and re-layouts: 56.5 us -> none  [the longest x32 55.5 us: local_terms(): model_c = lax.dynamic_index_in_dim(model, channel, 1, keepdims=False)]
    dynamic_slice x64 -> x0, local copies, waits for them, and re-layouts: 52.4 us -> none  [the longest x32 29.6 us: local(): numer, denom = lax.map(one, jnp.arange(channels, dtype=jnp.int32))]
  transfers between devices with their start and end apart: 9 -> 51, of which waited for: 7 -> 14; matrix products, arithmetic and copies ran while one was open for 0% -> 1% of each run, Pallas kernels for 0% -> 7%
where the time goes in v1:
time: 314 us; the launch traced here: 309 us
  Pallas kernels  164 us (52%)
  starting transfers between devices  99.7 us (32%)
  waiting for transfers between devices  25.3 us (8%)
  other arithmetic  14.1 us (4%)
  local copies, waits for them, and re-layouts  5.08 us (2%)
    pallas_call x4, Pallas kernels, sweep(): pl.pallas_call(functools.partial(kernel, first, final), out_shape=out_sha...  164 us
    ppermute x45, starting transfers between devices, move(): return lax.ppermute(block, GRID, pairs)  76.6 us
    ppermute x45, waiting for transfers between devices, move(): return lax.ppermute(block, GRID, pairs)  22.9 us
    ppermute x3, starting transfers between devices, smooth(): high = lax.ppermute(averaged[:, :, :, :reach], 'chan', backward)  13.3 us
    ppermute x3, starting transfers between devices, smooth(): low = lax.ppermute(averaged[:, :, :, channels - reach:], 'chan', forward)  9.74 us
    div x3, other arithmetic, smooth(): return total / coverage[:, None]  9.73 us
  transfers between devices with their start and end apart: 51, of which 14 were waited for; matrix products, arithmetic and copies ran while one was open for 1% of the time, Pallas kernels for 7%

profile of v1, /device:TPU:25, one launch (start us, length us, event | category | flops | bytes accessed | tf_op | source)
XLA Modules:
  0.0 309.3 jit_solution(1673807517262425182)
XLA Ops:
  0.7 1.6 copy-done
  2.3 1.0 copy-done.2
  3.3 1.0 copy-done.3
  4.4 0.7 copy-done.5
  5.1 47.9 %shard_map.104 = (f32[2,3,2,8,128]{4,3,2,1,0:T(8,128)S(1)}, f32[2,3,2,8,128]{4,3,2,1,0:T(8,128)S(1)}, f32[2,3,2,8,128]{4,3,2,1,0:T(8,128)S(1)}, f32[2,3,2,8,128]...) custom-call(s32[2]{0:T(128)S(1)} %pad_add_fusion.place, ...), custom_call_target="tpu_custom_call" | custom-call | flops 10000000000 | bytes 20000000 | tf_op jit(solution)/shard_map/pallas_call | solution.py:221
  53.1 1.7 collective-permute-start
  54.8 3.3 %collective-permute-start.1 = (f32[2,3,2,8,128]{4,3,2,1,0:T(8,128)S(1)}, f32[2,3,2,8,128]{4,3,2,1,0:T(8,128)S(1)}, u32[]{:S(2)}, u32[]{:S(2)}) collective-permute-start(f32[2,3,2,8,128]{4,3,2,1,0:T(8,128)S(1)} %get-tuple-element.28), channel_id=1, source_target_pairs={{0,16},{8,24},{16,0},{24,8},{32,48},{40,56},{48,32},{56,40},{64,80... | collective-permute-start | bytes 147464 | tf_op jit(solution)/shard_map/ppermute | solution.py:251
  58.1 0.7 collective-permute-start.2
  58.8 4.0 %collective-permute-start.3 = (f32[2,3,2,8,128]{4,3,2,1,0:T(8,128)S(1)}, f32[2,3,2,8,128]{4,3,2,1,0:T(8,128)S(1)}, u32[]{:S(2)}, u32[]{:S(2)}) collective-permute-start(f32[2,3,2,8,128]{4,3,2,1,0:T(8,128)S(1)} %get-tuple-element.30), channel_id=1, source_target_pairs={{0,0},{8,32},{16,64},{24,96},{32,8},{40,40},{48,72},{56,104},{64,1... | collective-permute-start | bytes 147464 | tf_op jit(solution)/shard_map/ppermute | solution.py:251
  62.8 3.5 %collective-permute-start.4 = (f32[2,3,2,8,128]{4,3,2,1,0:T(8,128)S(1)}, f32[2,3,2,8,128]{4,3,2,1,0:T(8,128)S(1)}, u32[]{:S(2)}, u32[]{:S(2)}) collective-permute-start(f32[2,3,2,8,128]{4,3,2,1,0:T(8,128)S(1)} %get-tuple-element.31), channel_id=1, source_target_pairs={{0,8},{8,40},{16,72},{24,104},{32,16},{40,48},{48,80},{56,112},{64... | collective-permute-start | bytes 147464 | tf_op jit(solution)/shard_map/ppermute | solution.py:251
  66.4 0.5 collective-permute-start.6
  66.9 0.7 fusion.46
  67.5 3.2 %collective-permute-done.5 = f32[2,3,2,8,128]{4,3,2,1,0:T(8,128)S(1)} collective-permute-done((f32[2,3,2,8,128]{4,3,2,1,0:T(8,128)S(1)}, f32[2,3,2,8,128]{4,3,2,1,0:T(8,128)S(1)}, u32[]{:S(2)}, u32[]{:S(2)}) %collective-permute-start.5) | collective-permute-done | bytes 49184 | tf_op jit(solution)/shard_map/ppermute | solution.py:251
  70.9 4.4 %collective-permute-start.7 = (f32[2,2,2,2,128]{4,3,2,1,0:T(2,128)S(1)}, f32[2,2,2,2,128]{4,3,2,1,0:T(2,128)S(1)}, u32[]{:S(2)}, u32[]{:S(2)}) collective-permute-start(f32[2,2,2,2,128]{4,3,2,1,0:T(2,128)S(1)} %get-tuple-element.62), channel_id=1, source_target_pairs={{0,1},{1,2},{2,3},{3,4},{4,5},{5,6},{6,7},{8,9},{9,10},{10,11},{11... | collective-permute-start | bytes 24584 | tf_op jit(solution)/shard_map/ppermute | solution.py:261
  75.2 3.3 %collective-permute-start.8 = (f32[2,2,2,2,128]{4,3,2,1,0:T(2,128)S(1)}, f32[2,2,2,2,128]{4,3,2,1,0:T(2,128)S(1)}, u32[]{:S(2)}, u32[]{:S(2)}) collective-permute-start(f32[2,2,2,2,128]{4,3,2,1,0:T(2,128)S(1)} %get-tuple-element.63), channel_id=1, source_target_pairs={{1,0},{2,1},{3,2},{4,3},{5,4},{6,5},{7,6},{9,8},{10,9},{11,10},{12... | collective-permute-start | bytes 24584 | tf_op jit(solution)/shard_map/ppermute | solution.py:262
  78.6 3.2 %fusion.42 = f32[8]{0:T(128)S(1)} fusion(f32[]{:T(128)} %bitcast.7, f32[]{:T(128)} %bitcast.6, f32[]{:T(128)} %bitcast.5, f32[]{:T(128)} %bitcast.4, f32[]{:T(128)} %bitcast, s32[]{:T(128)S(6)} %mul.143), kind=kLoop, calls=%fused_computation.84 | loop fusion | flops 232 | bytes 56 | tf_op jit(solution)/shard_map/add | solution.py:271
  81.8 3.2 %fusion.22.refs_4_ = f32[2,2,2,8,128]{4,3,2,1,0:T(8,128)S(1)} fusion(f32[2,2,2,8,128]{4,3,2,1,0:T(8,128)S(1)} %fusion.35, f32[2,2,2,2,128]{4,3,2,1,0:T(2,128)S(1)} %collective-permute-done.8, f32[2,2,2,2,128]{4,3,2,1,0:T(2,128)S(1)} %collective-permute-done.7, f32[8]{0:T(128)S(1)} %fusion.42, f32[]{:T(128)} %bitcast.7, f32[]{:T(128)} %bitcast.6, f32[]{:T(128)} %bitcast.5, ...), kind=kLoop, calls=%fused_computation.43 | loop fusion | flops 114688 | bytes 81972 | tf_op jit(solution)/shard_map/div | solution.py:272
  85.0 0.9 collective-permute-start.15
  85.9 3.1 %collective-permute-start.14 = (f32[2,2,2,8,128]{4,3,2,1,0:T(8,128)S(1)}, f32[2,2,2,8,128]{4,3,2,1,0:T(8,128)S(1)}, u32[]{:S(2)}, u32[]{:S(2)}) collective-permute-start(f32[2,2,2,8,128]{4,3,2,1,0:T(8,128)S(1)} %fusion.22.refs_4_), channel_id=1, source_target_pairs={{0,64},{8,96},{16,0},{24,32},{32,72},{40,104},{48,8},{56,40},{64,8... | collective-permute-start | bytes 98312 | tf_op jit(solution)/shard_map/ppermute | solution.py:251
  89.0 0.9 collective-permute-start.13
  89.9 1.9 collective-permute-start.12
  91.9 2.2 collective-permute-start.11
  94.1 0.7 collective-permute-start.9
  94.7 0.7 collective-permute-done.12.refs_8_
  95.4 3.0 collective-permute-done.10.refs_6_
  98.5 47.6 %shard_map.105 = (f32[2,3,2,8,128]{4,3,2,1,0:T(8,128)S(1)}, f32[2,3,2,8,128]{4,3,2,1,0:T(8,128)S(1)}, f32[2,3,2,8,128]{4,3,2,1,0:T(8,128)S(1)}, f32[2,3,2,8,128]...) custom-call(s32[2]{0:T(128)S(1)} %pad_add_fusion.place, ...), custom_call_target="tpu_custom_call" | custom-call | flops 10000000000 | bytes 20000000 | tf_op jit(solution)/shard_map/pallas_call | solution.py:221
  146.3 1.7 collective-permute-start.17
  148.0 1.7 collective-permute-start.18
  149.7 6.0 %collective-permute-start.19 = (f32[2,3,2,8,128]{4,3,2,1,0:T(8,128)S(1)}, f32[2,3,2,8,128]{4,3,2,1,0:T(8,128)S(1)}, u32[]{:S(2)}, u32[]{:S(2)}) collective-permute-start(f32[2,3,2,8,128]{4,3,2,1,0:T(8,128)S(1)} %get-tuple-element.38), channel_id=1, source_target_pairs={{0,0},{8,32},{16,64},{24,96},{32,8},{40,40},{48,72},{56,104},{64,1... | collective-permute-start | bytes 147464 | tf_op jit(solution)/shard_map/ppermute | solution.py:251
  155.7 2.9 collective-permute-start.20
  159.2 0.7 collective-permute-done.20
  159.9 3.2 %collective-permute-done.21 = f32[2,3,2,8,128]{4,3,2,1,0:T(8,128)S(1)} collective-permute-done((f32[2,3,2,8,128]{4,3,2,1,0:T(8,128)S(1)}, f32[2,3,2,8,128]{4,3,2,1,0:T(8,128)S(1)}, u32[]{:S(2)}, u32[]{:S(2)}) %collective-permute-start.21) | collective-permute-done | bytes 49184 | tf_op jit(solution)/shard_map/ppermute | solution.py:251
  163.2 3.5 %collective-permute-start.23 = (f32[2,2,2,2,128]{4,3,2,1,0:T(2,128)S(1)}, f32[2,2,2,2,128]{4,3,2,1,0:T(2,128)S(1)}, u32[]{:S(2)}, u32[]{:S(2)}) collective-permute-start(f32[2,2,2,2,128]{4,3,2,1,0:T(2,128)S(1)} %get-tuple-element.60), channel_id=1, source_target_pairs={{0,1},{1,2},{2,3},{3,4},{4,5},{5,6},{6,7},{8,9},{9,10},{10,11},{11... | collective-permute-start | bytes 24584 | tf_op jit(solution)/shard_map/ppermute | solution.py:261
  166.7 4.2 %collective-permute-start.24 = (f32[2,2,2,2,128]{4,3,2,1,0:T(2,128)S(1)}, f32[2,2,2,2,128]{4,3,2,1,0:T(2,128)S(1)}, u32[]{:S(2)}, u32[]{:S(2)}) collective-permute-start(f32[2,2,2,2,128]{4,3,2,1,0:T(2,128)S(1)} %get-tuple-element.61), channel_id=1, source_target_pairs={{1,0},{2,1},{3,2},{4,3},{5,4},{6,5},{7,6},{9,8},{10,9},{11,10},{12... | collective-permute-start | bytes 24584 | tf_op jit(solution)/shard_map/ppermute | solution.py:262
  170.9 1.7 collective-permute-done.24
  172.6 3.2 %fusion.13.refs_4_ = f32[2,2,2,8,128]{4,3,2,1,0:T(8,128)S(1)} fusion(f32[2,2,2,8,128]{4,3,2,1,0:T(8,128)S(1)} %fusion.32, f32[2,2,2,2,128]{4,3,2,1,0:T(2,128)S(1)} %collective-permute-done.24, f32[2,2,2,2,128]{4,3,2,1,0:T(2,128)S(1)} %collective-permute-done.23, f32[8]{0:T(128)S(1)} %fusion.42, f32[]{:T(128)} %bitcast.7, f32[]{:T(128)} %bitcast.6, ...), kind=kLoop, calls=%fused_computation.34 | loop fusion | flops 114688 | bytes 81972 | tf_op jit(solution)/shard_map/div | solution.py:272
  175.8 0.7 collective-permute-start.31
  176.5 4.0 %collective-permute-start.30 = (f32[2,2,2,8,128]{4,3,2,1,0:T(8,128)S(1)}, f32[2,2,2,8,128]{4,3,2,1,0:T(8,128)S(1)}, u32[]{:S(2)}, u32[]{:S(2)}) collective-permute-start(f32[2,2,2,8,128]{4,3,2,1,0:T(8,128)S(1)} %fusion.13.refs_4_), channel_id=1, source_target_pairs={{0,64},{8,96},{16,0},{24,32},{32,72},{40,104},{48,8},{56,40},{64,8... | collective-permute-start | bytes 98312 | tf_op jit(solution)/shard_map/ppermute | solution.py:251
  180.5 3.2 %collective-permute-start.29 = (f32[2,2,2,8,128]{4,3,2,1,0:T(8,128)S(1)}, f32[2,2,2,8,128]{4,3,2,1,0:T(8,128)S(1)}, u32[]{:S(2)}, u32[]{:S(2)}) collective-permute-start(f32[2,2,2,8,128]{4,3,2,1,0:T(8,128)S(1)} %fusion.13.refs_4_), channel_id=1, source_target_pairs={{0,32},{8,64},{16,96},{24,0},{32,40},{40,72},{48,104},{56,8},{64,4... | collective-permute-start | bytes 98312 | tf_op jit(solution)/shard_map/ppermute | solution.py:251
  183.7 1.9 collective-permute-start.28
  185.6 2.2 collective-permute-start.27
  187.8 0.7 collective-permute-start.25
  188.9 3.5 %collective-permute-done.26.refs_6_ = f32[2,2,2,8,128]{4,3,2,1,0:T(8,128)S(1)} collective-permute-done((f32[2,2,2,8,128]{4,3,2,1,0:T(8,128)S(1)}, f32[2,2,2,8,128]{4,3,2,1,0:T(8,128)S(1)}, u32[]{:S(2)}, u32[]{:S(2)}) %collective-permute-start.26) | collective-permute-done | bytes 32800 | tf_op jit(solution)/shard_map/ppermute | solution.py:251
  192.6 47.6 %shard_map.106 = (f32[2,3,2,8,128]{4,3,2,1,0:T(8,128)S(1)}, f32[2,3,2,8,128]{4,3,2,1,0:T(8,128)S(1)}, f32[2,3,2,8,128]{4,3,2,1,0:T(8,128)S(1)}, f32[2,3,2,8,128]...) custom-call(s32[2]{0:T(128)S(1)} %pad_add_fusion.place, ...), custom_call_target="tpu_custom_call" | custom-call | flops 10000000000 | bytes 20000000 | tf_op jit(solution)/shard_map/pallas_call | solution.py:221
  240.3 1.9 collective-permute-start.33
  242.1 1.1 collective-permute-start.34
  243.2 5.0 %collective-permute-start.35 = (f32[2,3,2,8,128]{4,3,2,1,0:T(8,128)S(1)}, f32[2,3,2,8,128]{4,3,2,1,0:T(8,128)S(1)}, u32[]{:S(2)}, u32[]{:S(2)}) collective-permute-start(f32[2,3,2,8,128]{4,3,2,1,0:T(8,128)S(1)} %get-tuple-element.46), channel_id=1, source_target_pairs={{0,0},{8,32},{16,64},{24,96},{32,8},{40,40},{48,72},{56,104},{64,1... | collective-permute-start | bytes 147464 | tf_op jit(solution)/shard_map/ppermute | solution.py:251
  248.2 3.4 %collective-permute-start.36 = (f32[2,3,2,8,128]{4,3,2,1,0:T(8,128)S(1)}, f32[2,3,2,8,128]{4,3,2,1,0:T(8,128)S(1)}, u32[]{:S(2)}, u32[]{:S(2)}) collective-permute-start(f32[2,3,2,8,128]{4,3,2,1,0:T(8,128)S(1)} %get-tuple-element.47), channel_id=1, source_target_pairs={{0,8},{8,40},{16,72},{24,104},{32,16},{40,48},{48,80},{56,112},{64... | collective-permute-start | bytes 147464 | tf_op jit(solution)/shard_map/ppermute | solution.py:251
  252.1 1.2 collective-permute-done.36
  253.3 2.7 collective-permute-done.37
  256.1 1.9 collective-permute-start.39
  258.0 5.8 %collective-permute-start.40 = (f32[2,2,2,2,128]{4,3,2,1,0:T(2,128)S(1)}, f32[2,2,2,2,128]{4,3,2,1,0:T(2,128)S(1)}, u32[]{:S(2)}, u32[]{:S(2)}) collective-permute-start(f32[2,2,2,2,128]{4,3,2,1,0:T(2,128)S(1)} %get-tuple-element.59), channel_id=1, source_target_pairs={{1,0},{2,1},{3,2},{4,3},{5,4},{6,5},{7,6},{9,8},{10,9},{11,10},{12... | collective-permute-start | bytes 24584 | tf_op jit(solution)/shard_map/ppermute | solution.py:262
  263.8 0.8 collective-permute-done.40
  264.6 3.2 %fusion.4.refs_4_ = f32[2,2,2,8,128]{4,3,2,1,0:T(8,128)S(1)} fusion(f32[2,2,2,8,128]{4,3,2,1,0:T(8,128)S(1)} %fusion.29, f32[2,2,2,2,128]{4,3,2,1,0:T(2,128)S(1)} %collective-permute-done.40, f32[2,2,2,2,128]{4,3,2,1,0:T(2,128)S(1)} %collective-permute-done.39, f32[8]{0:T(128)S(1)} %fusion.42, f32[]{:T(128)} %bitcast.7, f32[]{:T(128)} %bitcast.6, ...), kind=kLoop, calls=%fused_computation.25 | loop fusion | flops 114688 | bytes 81972 | tf_op jit(solution)/shard_map/div | solution.py:272
  267.8 1.1 collective-permute-start.43
  268.9 1.6 collective-permute-start.42
  270.6 0.8 collective-permute-start.41
  271.4 0.6 collective-permute-start.48
  272.0 6.7 %collective-permute-start.47 = (f32[2,2,2,8,128]{4,3,2,1,0:T(8,128)S(1)}, f32[2,2,2,8,128]{4,3,2,1,0:T(8,128)S(1)}, u32[]{:S(2)}, u32[]{:S(2)}) collective-permute-start(f32[2,2,2,8,128]{4,3,2,1,0:T(8,128)S(1)} %fusion.4.refs_4_), channel_id=1, source_target_pairs={{0,0},{8,32},{16,64},{24,96},{32,8},{40,40},{48,72},{56,104},{64,1... | collective-permute-start | bytes 98312 | tf_op jit(solution)/shard_map/ppermute | solution.py:251
  278.8 3.9 %collective-permute-start.50 = (f32[2,2,2,8,128]{4,3,2,1,0:T(8,128)S(1)}, f32[2,2,2,8,128]{4,3,2,1,0:T(8,128)S(1)}, u32[]{:S(2)}, u32[]{:S(2)}) collective-permute-start(f32[2,2,2,8,128]{4,3,2,1,0:T(8,128)S(1)} %fusion.4.refs_4_), channel_id=1, source_target_pairs={{0,96},{8,0},{16,32},{24,64},{32,104},{40,8},{48,40},{56,72},{64,1... | collective-permute-start | bytes 98312 | tf_op jit(solution)/shard_map/ppermute | solution.py:251
  282.9 0.6 collective-permute-start.45
  283.8 3.5 %collective-permute-done.49.refs_10_ = f32[2,2,2,8,128]{4,3,2,1,0:T(8,128)S(1)} collective-permute-done((f32[2,2,2,8,128]{4,3,2,1,0:T(8,128)S(1)}, f32[2,2,2,8,128]{4,3,2,1,0:T(8,128)S(1)}, u32[]{:S(2)}, u32[]{:S(2)}) %collective-permute-start.49) | collective-permute-done | bytes 32800 | tf_op jit(solution)/shard_map/ppermute | solution.py:251
  287.3 21.0 %shard_map.107 = bf16[8,1,4,2,128,128]{5,4,3,2,1,0:T(8,128)(2,1)} custom-call(s32[2]{0:T(128)S(1)} %pad_add_fusion.place, bf16[8,8,1,4,2,128,128]{6,5,4,3,2,1,0:T(8,128)(2,1)} %refs_0_.7, bf16[8,1,4,2,128,128]{5,4,3,2,1,0:T(8,128)(2,1)S(1)} %copy-done.1, s32[8,128,128]{2,1,0:T(8,128)S(1)} %copy-done.4, bf16[16,512]{1,0:T(8,128)(2,1)S(1)} %copy-done.6, ...), custom_call_target="tpu_custom_call" | custom-call | flops 10000000000 | bytes 20000000 | tf_op jit(solution)/shard_map/pallas_call | solution.py:221
  308.4 0.8 pad_maximum_fusion
  (81 shorter events, 2.9 us)
Async XLA Ops:
  0.7 1.6 copy-start
  2.3 1.0 copy-start.2
  3.3 1.0 copy-start.3
  4.4 0.7 copy-start.5
  5.1 61.7 %copy-start.7 = (f32[5]{0:T(128)S(1)}, f32[5]{0:T(128)}, u32[]{:S(2)}) copy-start(f32[5]{0:T(128)} %param.13) | copy-start | bytes 64
  5.1 93.4 %copy-start.1 = (bf16[8,1,4,2,128,128]{5,4,3,2,1,0:T(8,128)(2,1)S(1)}, bf16[8,1,4,2,128,128]{5,4,3,2,1,0:T(8,128)(2,1)}, u32[]{:S(2)}) copy-start(bf16[8,1,4,2,128,128]{5,4,3,2,1,0:T(8,128)(2,1)} %refs_1_.7) | copy-start | bytes 6291460
  5.1 93.4 %copy-start.4 = (s32[8,128,128]{2,1,0:T(8,128)S(1)}, s32[8,128,128]{2,1,0:T(8,128)}, u32[]{:S(2)}) copy-start(s32[8,128,128]{2,1,0:T(8,128)} %refs_2_.7) | copy-start | bytes 1572868
  5.1 93.4 %copy-start.6 = (bf16[16,512]{1,0:T(8,128)(2,1)S(1)}, bf16[16,512]{1,0:T(8,128)(2,1)}, u32[]{:S(2)}) copy-start(bf16[16,512]{1,0:T(8,128)(2,1)} %constant.77.clone.refs_3_) | copy-start | bytes 49156
  53.1 13.3 %collective-permute-start = (f32[2,3,2,8,128]{4,3,2,1,0:T(8,128)S(1)}, f32[2,3,2,8,128]{4,3,2,1,0:T(8,128)S(1)}, u32[]{:S(2)}, u32[]{:S(2)}) collective-permute-start(f32[2,3,2,8,128]{4,3,2,1,0:T(8,128)S(1)} %get-tuple-element.27), channel_id=1, source_target_pairs={{0,8},{8,16},{16,24},{24,0},{32,40},{40,48},{48,56},{56,32},{64,72... | collective-permute-start | bytes 147464 | tf_op jit(solution)/shard_map/ppermute | solution.py:251
  54.8 11.6 %collective-permute-start.1 = (f32[2,3,2,8,128]{4,3,2,1,0:T(8,128)S(1)}, f32[2,3,2,8,128]{4,3,2,1,0:T(8,128)S(1)}, u32[]{:S(2)}, u32[]{:S(2)}) collective-permute-start(f32[2,3,2,8,128]{4,3,2,1,0:T(8,128)S(1)} %get-tuple-element.28), channel_id=1, source_target_pairs={{0,16},{8,24},{16,0},{24,8},{32,48},{40,56},{48,32},{56,40},{64,80... | collective-permute-start | bytes 147464 | tf_op jit(solution)/shard_map/ppermute | solution.py:251
  58.1 9.4 %collective-permute-start.2 = (f32[2,3,2,8,128]{4,3,2,1,0:T(8,128)S(1)}, f32[2,3,2,8,128]{4,3,2,1,0:T(8,128)S(1)}, u32[]{:S(2)}, u32[]{:S(2)}) collective-permute-start(f32[2,3,2,8,128]{4,3,2,1,0:T(8,128)S(1)} %get-tuple-element.29), channel_id=1, source_target_pairs={{0,24},{8,0},{16,8},{24,16},{32,56},{40,32},{48,40},{56,48},{64,88... | collective-permute-start | bytes 147464 | tf_op jit(solution)/shard_map/ppermute | solution.py:251
  58.8 8.7 %collective-permute-start.3 = (f32[2,3,2,8,128]{4,3,2,1,0:T(8,128)S(1)}, f32[2,3,2,8,128]{4,3,2,1,0:T(8,128)S(1)}, u32[]{:S(2)}, u32[]{:S(2)}) collective-permute-start(f32[2,3,2,8,128]{4,3,2,1,0:T(8,128)S(1)} %get-tuple-element.30), channel_id=1, source_target_pairs={{0,0},{8,32},{16,64},{24,96},{32,8},{40,40},{48,72},{56,104},{64,1... | collective-permute-start | bytes 147464 | tf_op jit(solution)/shard_map/ppermute | solution.py:251
  62.8 4.7 %collective-permute-start.4 = (f32[2,3,2,8,128]{4,3,2,1,0:T(8,128)S(1)}, f32[2,3,2,8,128]{4,3,2,1,0:T(8,128)S(1)}, u32[]{:S(2)}, u32[]{:S(2)}) collective-permute-start(f32[2,3,2,8,128]{4,3,2,1,0:T(8,128)S(1)} %get-tuple-element.31), channel_id=1, source_target_pairs={{0,8},{8,40},{16,72},{24,104},{32,16},{40,48},{48,80},{56,112},{64... | collective-permute-start | bytes 147464 | tf_op jit(solution)/shard_map/ppermute | solution.py:251
  66.4 4.4 %collective-permute-start.5 = (f32[2,3,2,8,128]{4,3,2,1,0:T(8,128)S(1)}, f32[2,3,2,8,128]{4,3,2,1,0:T(8,128)S(1)}, u32[]{:S(2)}, u32[]{:S(2)}) collective-permute-start(f32[2,3,2,8,128]{4,3,2,1,0:T(8,128)S(1)} %get-tuple-element.32), channel_id=1, source_target_pairs={{0,16},{8,48},{16,80},{24,112},{32,24},{40,56},{48,88},{56,120},{6... | collective-permute-start | bytes 147464 | tf_op jit(solution)/shard_map/ppermute | solution.py:251
  66.4 4.4 %collective-permute-start.6 = (f32[2,3,2,8,128]{4,3,2,1,0:T(8,128)S(1)}, f32[2,3,2,8,128]{4,3,2,1,0:T(8,128)S(1)}, u32[]{:S(2)}, u32[]{:S(2)}) collective-permute-start(f32[2,3,2,8,128]{4,3,2,1,0:T(8,128)S(1)} %get-tuple-element.33), channel_id=1, source_target_pairs={{0,24},{8,56},{16,88},{24,120},{32,0},{40,32},{48,64},{56,96},{64,... | collective-permute-start | bytes 147464 | tf_op jit(solution)/shard_map/ppermute | solution.py:251
  70.9 10.9 %collective-permute-start.7 = (f32[2,2,2,2,128]{4,3,2,1,0:T(2,128)S(1)}, f32[2,2,2,2,128]{4,3,2,1,0:T(2,128)S(1)}, u32[]{:S(2)}, u32[]{:S(2)}) collective-permute-start(f32[2,2,2,2,128]{4,3,2,1,0:T(2,128)S(1)} %get-tuple-element.62), channel_id=1, source_target_pairs={{0,1},{1,2},{2,3},{3,4},{4,5},{5,6},{6,7},{8,9},{9,10},{10,11},{11... | collective-permute-start | bytes 24584 | tf_op jit(solution)/shard_map/ppermute | solution.py:261
  75.2 6.5 %collective-permute-start.8 = (f32[2,2,2,2,128]{4,3,2,1,0:T(2,128)S(1)}, f32[2,2,2,2,128]{4,3,2,1,0:T(2,128)S(1)}, u32[]{:S(2)}, u32[]{:S(2)}) collective-permute-start(f32[2,2,2,2,128]{4,3,2,1,0:T(2,128)S(1)} %get-tuple-element.63), channel_id=1, source_target_pairs={{1,0},{2,1},{3,2},{4,3},{5,4},{6,5},{7,6},{9,8},{10,9},{11,10},{12... | collective-permute-start | bytes 24584 | tf_op jit(solution)/shard_map/ppermute | solution.py:262
  85.0 9.1 %collective-permute-start.15 = (f32[2,2,2,8,128]{4,3,2,1,0:T(8,128)S(1)}, f32[2,2,2,8,128]{4,3,2,1,0:T(8,128)S(1)}, u32[]{:S(2)}, u32[]{:S(2)}) collective-permute-start(f32[2,2,2,8,128]{4,3,2,1,0:T(8,128)S(1)} %fusion.22.refs_4_), channel_id=1, source_target_pairs={{0,96},{8,0},{16,32},{24,64},{32,104},{40,8},{48,40},{56,72},{64,1... | collective-permute-start | bytes 98312 | tf_op jit(solution)/shard_map/ppermute | solution.py:251
  85.9 8.1 %collective-permute-start.14 = (f32[2,2,2,8,128]{4,3,2,1,0:T(8,128)S(1)}, f32[2,2,2,8,128]{4,3,2,1,0:T(8,128)S(1)}, u32[]{:S(2)}, u32[]{:S(2)}) collective-permute-start(f32[2,2,2,8,128]{4,3,2,1,0:T(8,128)S(1)} %fusion.22.refs_4_), channel_id=1, source_target_pairs={{0,64},{8,96},{16,0},{24,32},{32,72},{40,104},{48,8},{56,40},{64,8... | collective-permute-start | bytes 98312 | tf_op jit(solution)/shard_map/ppermute | solution.py:251
  89.0 5.7 %collective-permute-start.13 = (f32[2,2,2,8,128]{4,3,2,1,0:T(8,128)S(1)}, f32[2,2,2,8,128]{4,3,2,1,0:T(8,128)S(1)}, u32[]{:S(2)}, u32[]{:S(2)}) collective-permute-start(f32[2,2,2,8,128]{4,3,2,1,0:T(8,128)S(1)} %fusion.22.refs_4_), channel_id=1, source_target_pairs={{0,32},{8,64},{16,96},{24,0},{32,40},{40,72},{48,104},{56,8},{64,4... | collective-permute-start | bytes 98312 | tf_op jit(solution)/shard_map/ppermute | solution.py:251
  89.9 5.5 %collective-permute-start.12 = (f32[2,2,2,8,128]{4,3,2,1,0:T(8,128)S(1)}, f32[2,2,2,8,128]{4,3,2,1,0:T(8,128)S(1)}, u32[]{:S(2)}, u32[]{:S(2)}) collective-permute-start(f32[2,2,2,8,128]{4,3,2,1,0:T(8,128)S(1)} %fusion.22.refs_4_), channel_id=1, source_target_pairs={{0,0},{8,32},{16,64},{24,96},{32,8},{40,40},{48,72},{56,104},{64,1... | collective-permute-start | bytes 98312 | tf_op jit(solution)/shard_map/ppermute | solution.py:251
  91.9 3.5 %collective-permute-start.11 = (f32[2,2,2,8,128]{4,3,2,1,0:T(8,128)S(1)}, f32[2,2,2,8,128]{4,3,2,1,0:T(8,128)S(1)}, u32[]{:S(2)}, u32[]{:S(2)}) collective-permute-start(f32[2,2,2,8,128]{4,3,2,1,0:T(8,128)S(1)} %fusion.22.refs_4_), channel_id=1, source_target_pairs={{0,24},{8,0},{16,8},{24,16},{32,56},{40,32},{48,40},{56,48},{64,88... | collective-permute-start | bytes 98312 | tf_op jit(solution)/shard_map/ppermute | solution.py:251
  94.1 4.4 %collective-permute-start.10 = (f32[2,2,2,8,128]{4,3,2,1,0:T(8,128)S(1)}, f32[2,2,2,8,128]{4,3,2,1,0:T(8,128)S(1)}, u32[]{:S(2)}, u32[]{:S(2)}) collective-permute-start(f32[2,2,2,8,128]{4,3,2,1,0:T(8,128)S(1)} %fusion.22.refs_4_), channel_id=1, source_target_pairs={{0,16},{8,24},{16,0},{24,8},{32,48},{40,56},{48,32},{56,40},{64,80... | collective-permute-start | bytes 98312 | tf_op jit(solution)/shard_map/ppermute | solution.py:251
  94.1 4.4 %collective-permute-start.9 = (f32[2,2,2,8,128]{4,3,2,1,0:T(8,128)S(1)}, f32[2,2,2,8,128]{4,3,2,1,0:T(8,128)S(1)}, u32[]{:S(2)}, u32[]{:S(2)}) collective-permute-start(f32[2,2,2,8,128]{4,3,2,1,0:T(8,128)S(1)} %fusion.22.refs_4_), channel_id=1, source_target_pairs={{0,8},{8,16},{16,24},{24,0},{32,40},{40,48},{48,56},{56,32},{64,72... | collective-permute-start | bytes 98312 | tf_op jit(solution)/shard_map/ppermute | solution.py:251
  146.1 12.6 %collective-permute-start.16 = (f32[2,3,2,8,128]{4,3,2,1,0:T(8,128)S(1)}, f32[2,3,2,8,128]{4,3,2,1,0:T(8,128)S(1)}, u32[]{:S(2)}, u32[]{:S(2)}) collective-permute-start(f32[2,3,2,8,128]{4,3,2,1,0:T(8,128)S(1)} %get-tuple-element.35), channel_id=1, source_target_pairs={{0,8},{8,16},{16,24},{24,0},{32,40},{40,48},{48,56},{56,32},{64,72... | collective-permute-start | bytes 147464 | tf_op jit(solution)/shard_map/ppermute | solution.py:251
  146.3 12.4 %collective-permute-start.17 = (f32[2,3,2,8,128]{4,3,2,1,0:T(8,128)S(1)}, f32[2,3,2,8,128]{4,3,2,1,0:T(8,128)S(1)}, u32[]{:S(2)}, u32[]{:S(2)}) collective-permute-start(f32[2,3,2,8,128]{4,3,2,1,0:T(8,128)S(1)} %get-tuple-element.36), channel_id=1, source_target_pairs={{0,16},{8,24},{16,0},{24,8},{32,48},{40,56},{48,32},{56,40},{64,80... | collective-permute-start | bytes 147464 | tf_op jit(solution)/shard_map/ppermute | solution.py:251
  148.0 11.2 %collective-permute-start.18 = (f32[2,3,2,8,128]{4,3,2,1,0:T(8,128)S(1)}, f32[2,3,2,8,128]{4,3,2,1,0:T(8,128)S(1)}, u32[]{:S(2)}, u32[]{:S(2)}) collective-permute-start(f32[2,3,2,8,128]{4,3,2,1,0:T(8,128)S(1)} %get-tuple-element.37), channel_id=1, source_target_pairs={{0,24},{8,0},{16,8},{24,16},{32,56},{40,32},{48,40},{56,48},{64,88... | collective-permute-start | bytes 147464 | tf_op jit(solution)/shard_map/ppermute | solution.py:251
  149.7 9.5 %collective-permute-start.19 = (f32[2,3,2,8,128]{4,3,2,1,0:T(8,128)S(1)}, f32[2,3,2,8,128]{4,3,2,1,0:T(8,128)S(1)}, u32[]{:S(2)}, u32[]{:S(2)}) collective-permute-start(f32[2,3,2,8,128]{4,3,2,1,0:T(8,128)S(1)} %get-tuple-element.38), channel_id=1, source_target_pairs={{0,0},{8,32},{16,64},{24,96},{32,8},{40,40},{48,72},{56,104},{64,1... | collective-permute-start | bytes 147464 | tf_op jit(solution)/shard_map/ppermute | solution.py:251
  155.7 4.2 %collective-permute-start.20 = (f32[2,3,2,8,128]{4,3,2,1,0:T(8,128)S(1)}, f32[2,3,2,8,128]{4,3,2,1,0:T(8,128)S(1)}, u32[]{:S(2)}, u32[]{:S(2)}) collective-permute-start(f32[2,3,2,8,128]{4,3,2,1,0:T(8,128)S(1)} %get-tuple-element.39), channel_id=1, source_target_pairs={{0,8},{8,40},{16,72},{24,104},{32,16},{40,48},{48,80},{56,112},{64... | collective-permute-start | bytes 147464 | tf_op jit(solution)/shard_map/ppermute | solution.py:251
  158.7 4.4 %collective-permute-start.21 = (f32[2,3,2,8,128]{4,3,2,1,0:T(8,128)S(1)}, f32[2,3,2,8,128]{4,3,2,1,0:T(8,128)S(1)}, u32[]{:S(2)}, u32[]{:S(2)}) collective-permute-start(f32[2,3,2,8,128]{4,3,2,1,0:T(8,128)S(1)} %get-tuple-element.40), channel_id=1, source_target_pairs={{0,16},{8,48},{16,80},{24,112},{32,24},{40,56},{48,88},{56,120},{6... | collective-permute-start | bytes 147464 | tf_op jit(solution)/shard_map/ppermute | solution.py:251
  158.7 4.4 %collective-permute-start.22 = (f32[2,3,2,8,128]{4,3,2,1,0:T(8,128)S(1)}, f32[2,3,2,8,128]{4,3,2,1,0:T(8,128)S(1)}, u32[]{:S(2)}, u32[]{:S(2)}) collective-permute-start(f32[2,3,2,8,128]{4,3,2,1,0:T(8,128)S(1)} %get-tuple-element.41), channel_id=1, source_target_pairs={{0,24},{8,56},{16,88},{24,120},{32,0},{40,32},{48,64},{56,96},{64,... | collective-permute-start | bytes 147464 | tf_op jit(solution)/shard_map/ppermute | solution.py:251
  163.2 7.7 %collective-permute-start.23 = (f32[2,2,2,2,128]{4,3,2,1,0:T(2,128)S(1)}, f32[2,2,2,2,128]{4,3,2,1,0:T(2,128)S(1)}, u32[]{:S(2)}, u32[]{:S(2)}) collective-permute-start(f32[2,2,2,2,128]{4,3,2,1,0:T(2,128)S(1)} %get-tuple-element.60), channel_id=1, source_target_pairs={{0,1},{1,2},{2,3},{3,4},{4,5},{5,6},{6,7},{8,9},{9,10},{10,11},{11... | collective-permute-start | bytes 24584 | tf_op jit(solution)/shard_map/ppermute | solution.py:261
  166.7 5.9 %collective-permute-start.24 = (f32[2,2,2,2,128]{4,3,2,1,0:T(2,128)S(1)}, f32[2,2,2,2,128]{4,3,2,1,0:T(2,128)S(1)}, u32[]{:S(2)}, u32[]{:S(2)}) collective-permute-start(f32[2,2,2,2,128]{4,3,2,1,0:T(2,128)S(1)} %get-tuple-element.61), channel_id=1, source_target_pairs={{1,0},{2,1},{3,2},{4,3},{5,4},{6,5},{7,6},{9,8},{10,9},{11,10},{12... | collective-permute-start | bytes 24584 | tf_op jit(solution)/shard_map/ppermute | solution.py:262
  175.8 12.0 %collective-permute-start.31 = (f32[2,2,2,8,128]{4,3,2,1,0:T(8,128)S(1)}, f32[2,2,2,8,128]{4,3,2,1,0:T(8,128)S(1)}, u32[]{:S(2)}, u32[]{:S(2)}) collective-permute-start(f32[2,2,2,8,128]{4,3,2,1,0:T(8,128)S(1)} %fusion.13.refs_4_), channel_id=1, source_target_pairs={{0,96},{8,0},{16,32},{24,64},{32,104},{40,8},{48,40},{56,72},{64,1... | collective-permute-start | bytes 98312 | tf_op jit(solution)/shard_map/ppermute | solution.py:251
  176.5 11.3 %collective-permute-start.30 = (f32[2,2,2,8,128]{4,3,2,1,0:T(8,128)S(1)}, f32[2,2,2,8,128]{4,3,2,1,0:T(8,128)S(1)}, u32[]{:S(2)}, u32[]{:S(2)}) collective-permute-start(f32[2,2,2,8,128]{4,3,2,1,0:T(8,128)S(1)} %fusion.13.refs_4_), channel_id=1, source_target_pairs={{0,64},{8,96},{16,0},{24,32},{32,72},{40,104},{48,8},{56,40},{64,8... | collective-permute-start | bytes 98312 | tf_op jit(solution)/shard_map/ppermute | solution.py:251
  180.5 8.0 %collective-permute-start.29 = (f32[2,2,2,8,128]{4,3,2,1,0:T(8,128)S(1)}, f32[2,2,2,8,128]{4,3,2,1,0:T(8,128)S(1)}, u32[]{:S(2)}, u32[]{:S(2)}) collective-permute-start(f32[2,2,2,8,128]{4,3,2,1,0:T(8,128)S(1)} %fusion.13.refs_4_), channel_id=1, source_target_pairs={{0,32},{8,64},{16,96},{24,0},{32,40},{40,72},{48,104},{56,8},{64,4... | collective-permute-start | bytes 98312 | tf_op jit(solution)/shard_map/ppermute | solution.py:251
  183.7 5.2 %collective-permute-start.28 = (f32[2,2,2,8,128]{4,3,2,1,0:T(8,128)S(1)}, f32[2,2,2,8,128]{4,3,2,1,0:T(8,128)S(1)}, u32[]{:S(2)}, u32[]{:S(2)}) collective-permute-start(f32[2,2,2,8,128]{4,3,2,1,0:T(8,128)S(1)} %fusion.13.refs_4_), channel_id=1, source_target_pairs={{0,0},{8,32},{16,64},{24,96},{32,8},{40,40},{48,72},{56,104},{64,1... | collective-permute-start | bytes 98312 | tf_op jit(solution)/shard_map/ppermute | solution.py:251
  185.6 3.3 %collective-permute-start.27 = (f32[2,2,2,8,128]{4,3,2,1,0:T(8,128)S(1)}, f32[2,2,2,8,128]{4,3,2,1,0:T(8,128)S(1)}, u32[]{:S(2)}, u32[]{:S(2)}) collective-permute-start(f32[2,2,2,8,128]{4,3,2,1,0:T(8,128)S(1)} %fusion.13.refs_4_), channel_id=1, source_target_pairs={{0,24},{8,0},{16,8},{24,16},{32,56},{40,32},{48,40},{56,48},{64,88... | collective-permute-start | bytes 98312 | tf_op jit(solution)/shard_map/ppermute | solution.py:251
  187.8 4.6 %collective-permute-start.26 = (f32[2,2,2,8,128]{4,3,2,1,0:T(8,128)S(1)}, f32[2,2,2,8,128]{4,3,2,1,0:T(8,128)S(1)}, u32[]{:S(2)}, u32[]{:S(2)}) collective-permute-start(f32[2,2,2,8,128]{4,3,2,1,0:T(8,128)S(1)} %fusion.13.refs_4_), channel_id=1, source_target_pairs={{0,16},{8,24},{16,0},{24,8},{32,48},{40,56},{48,32},{56,40},{64,80... | collective-permute-start | bytes 98312 | tf_op jit(solution)/shard_map/ppermute | solution.py:251
  187.8 4.8 %collective-permute-start.25 = (f32[2,2,2,8,128]{4,3,2,1,0:T(8,128)S(1)}, f32[2,2,2,8,128]{4,3,2,1,0:T(8,128)S(1)}, u32[]{:S(2)}, u32[]{:S(2)}) collective-permute-start(f32[2,2,2,8,128]{4,3,2,1,0:T(8,128)S(1)} %fusion.13.refs_4_), channel_id=1, source_target_pairs={{0,8},{8,16},{16,24},{24,0},{32,40},{40,48},{48,56},{56,32},{64,72... | collective-permute-start | bytes 98312 | tf_op jit(solution)/shard_map/ppermute | solution.py:251
  240.2 11.4 %collective-permute-start.32 = (f32[2,3,2,8,128]{4,3,2,1,0:T(8,128)S(1)}, f32[2,3,2,8,128]{4,3,2,1,0:T(8,128)S(1)}, u32[]{:S(2)}, u32[]{:S(2)}) collective-permute-start(f32[2,3,2,8,128]{4,3,2,1,0:T(8,128)S(1)} %get-tuple-element.43), channel_id=1, source_target_pairs={{0,8},{8,16},{16,24},{24,0},{32,40},{40,48},{48,56},{56,32},{64,72... | collective-permute-start | bytes 147464 | tf_op jit(solution)/shard_map/ppermute | solution.py:251
  240.3 11.3 %collective-permute-start.33 = (f32[2,3,2,8,128]{4,3,2,1,0:T(8,128)S(1)}, f32[2,3,2,8,128]{4,3,2,1,0:T(8,128)S(1)}, u32[]{:S(2)}, u32[]{:S(2)}) collective-permute-start(f32[2,3,2,8,128]{4,3,2,1,0:T(8,128)S(1)} %get-tuple-element.44), channel_id=1, source_target_pairs={{0,16},{8,24},{16,0},{24,8},{32,48},{40,56},{48,32},{56,40},{64,80... | collective-permute-start | bytes 147464 | tf_op jit(solution)/shard_map/ppermute | solution.py:251
  242.1 10.0 %collective-permute-start.34 = (f32[2,3,2,8,128]{4,3,2,1,0:T(8,128)S(1)}, f32[2,3,2,8,128]{4,3,2,1,0:T(8,128)S(1)}, u32[]{:S(2)}, u32[]{:S(2)}) collective-permute-start(f32[2,3,2,8,128]{4,3,2,1,0:T(8,128)S(1)} %get-tuple-element.45), channel_id=1, source_target_pairs={{0,24},{8,0},{16,8},{24,16},{32,56},{40,32},{48,40},{56,48},{64,88... | collective-permute-start | bytes 147464 | tf_op jit(solution)/shard_map/ppermute | solution.py:251
  243.2 8.9 %collective-permute-start.35 = (f32[2,3,2,8,128]{4,3,2,1,0:T(8,128)S(1)}, f32[2,3,2,8,128]{4,3,2,1,0:T(8,128)S(1)}, u32[]{:S(2)}, u32[]{:S(2)}) collective-permute-start(f32[2,3,2,8,128]{4,3,2,1,0:T(8,128)S(1)} %get-tuple-element.46), channel_id=1, source_target_pairs={{0,0},{8,32},{16,64},{24,96},{32,8},{40,40},{48,72},{56,104},{64,1... | collective-permute-start | bytes 147464 | tf_op jit(solution)/shard_map/ppermute | solution.py:251
  248.2 5.1 %collective-permute-start.36 = (f32[2,3,2,8,128]{4,3,2,1,0:T(8,128)S(1)}, f32[2,3,2,8,128]{4,3,2,1,0:T(8,128)S(1)}, u32[]{:S(2)}, u32[]{:S(2)}) collective-permute-start(f32[2,3,2,8,128]{4,3,2,1,0:T(8,128)S(1)} %get-tuple-element.47), channel_id=1, source_target_pairs={{0,8},{8,40},{16,72},{24,104},{32,16},{40,48},{48,80},{56,112},{64... | collective-permute-start | bytes 147464 | tf_op jit(solution)/shard_map/ppermute | solution.py:251
  251.6 4.4 %collective-permute-start.37 = (f32[2,3,2,8,128]{4,3,2,1,0:T(8,128)S(1)}, f32[2,3,2,8,128]{4,3,2,1,0:T(8,128)S(1)}, u32[]{:S(2)}, u32[]{:S(2)}) collective-permute-start(f32[2,3,2,8,128]{4,3,2,1,0:T(8,128)S(1)} %get-tuple-element.48), channel_id=1, source_target_pairs={{0,16},{8,48},{16,80},{24,112},{32,24},{40,56},{48,88},{56,120},{6... | collective-permute-start | bytes 147464 | tf_op jit(solution)/shard_map/ppermute | solution.py:251
  251.6 4.4 %collective-permute-start.38 = (f32[2,3,2,8,128]{4,3,2,1,0:T(8,128)S(1)}, f32[2,3,2,8,128]{4,3,2,1,0:T(8,128)S(1)}, u32[]{:S(2)}, u32[]{:S(2)}) collective-permute-start(f32[2,3,2,8,128]{4,3,2,1,0:T(8,128)S(1)} %get-tuple-element.49), channel_id=1, source_target_pairs={{0,24},{8,56},{16,88},{24,120},{32,0},{40,32},{48,64},{56,96},{64,... | collective-permute-start | bytes 147464 | tf_op jit(solution)/shard_map/ppermute | solution.py:251
  256.1 7.7 %collective-permute-start.39 = (f32[2,2,2,2,128]{4,3,2,1,0:T(2,128)S(1)}, f32[2,2,2,2,128]{4,3,2,1,0:T(2,128)S(1)}, u32[]{:S(2)}, u32[]{:S(2)}) collective-permute-start(f32[2,2,2,2,128]{4,3,2,1,0:T(2,128)S(1)} %get-tuple-element.58), channel_id=1, source_target_pairs={{0,1},{1,2},{2,3},{3,4},{4,5},{5,6},{6,7},{8,9},{9,10},{10,11},{11... | collective-permute-start | bytes 24584 | tf_op jit(solution)/shard_map/ppermute | solution.py:261
  258.0 6.5 %collective-permute-start.40 = (f32[2,2,2,2,128]{4,3,2,1,0:T(2,128)S(1)}, f32[2,2,2,2,128]{4,3,2,1,0:T(2,128)S(1)}, u32[]{:S(2)}, u32[]{:S(2)}) collective-permute-start(f32[2,2,2,2,128]{4,3,2,1,0:T(2,128)S(1)} %get-tuple-element.59), channel_id=1, source_target_pairs={{1,0},{2,1},{3,2},{4,3},{5,4},{6,5},{7,6},{9,8},{10,9},{11,10},{12... | collective-permute-start | bytes 24584 | tf_op jit(solution)/shard_map/ppermute | solution.py:262
  267.8 11.0 %collective-permute-start.43 = (f32[2,2,2,8,128]{4,3,2,1,0:T(8,128)S(1)}, f32[2,2,2,8,128]{4,3,2,1,0:T(8,128)S(1)}, u32[]{:S(2)}, u32[]{:S(2)}) collective-permute-start(f32[2,2,2,8,128]{4,3,2,1,0:T(8,128)S(1)} %fusion.4.refs_4_), channel_id=1, source_target_pairs={{0,8},{8,16},{16,24},{24,0},{32,40},{40,48},{48,56},{56,32},{64,72... | collective-permute-start | bytes 98312 | tf_op jit(solution)/shard_map/ppermute | solution.py:251
  268.9 13.8 %collective-permute-start.42 = (f32[2,2,2,8,128]{4,3,2,1,0:T(8,128)S(1)}, f32[2,2,2,8,128]{4,3,2,1,0:T(8,128)S(1)}, u32[]{:S(2)}, u32[]{:S(2)}) collective-permute-start(f32[2,2,2,8,128]{4,3,2,1,0:T(8,128)S(1)} %fusion.4.refs_4_), channel_id=1, source_target_pairs={{0,16},{8,24},{16,0},{24,8},{32,48},{40,56},{48,32},{56,40},{64,80... | collective-permute-start | bytes 98312 | tf_op jit(solution)/shard_map/ppermute | solution.py:251
  270.6 12.2 %collective-permute-start.41 = (f32[2,2,2,8,128]{4,3,2,1,0:T(8,128)S(1)}, f32[2,2,2,8,128]{4,3,2,1,0:T(8,128)S(1)}, u32[]{:S(2)}, u32[]{:S(2)}) collective-permute-start(f32[2,2,2,8,128]{4,3,2,1,0:T(8,128)S(1)} %fusion.4.refs_4_), channel_id=1, source_target_pairs={{0,24},{8,0},{16,8},{24,16},{32,56},{40,32},{48,40},{56,48},{64,88... | collective-permute-start | bytes 98312 | tf_op jit(solution)/shard_map/ppermute | solution.py:251
  271.4 11.5 %collective-permute-start.48 = (f32[2,2,2,8,128]{4,3,2,1,0:T(8,128)S(1)}, f32[2,2,2,8,128]{4,3,2,1,0:T(8,128)S(1)}, u32[]{:S(2)}, u32[]{:S(2)}) collective-permute-start(f32[2,2,2,8,128]{4,3,2,1,0:T(8,128)S(1)} %fusion.4.refs_4_), channel_id=1, source_target_pairs={{0,32},{8,64},{16,96},{24,0},{32,40},{40,72},{48,104},{56,8},{64,4... | collective-permute-start | bytes 98312 | tf_op jit(solution)/shard_map/ppermute | solution.py:251
  272.0 11.4 %collective-permute-start.47 = (f32[2,2,2,8,128]{4,3,2,1,0:T(8,128)S(1)}, f32[2,2,2,8,128]{4,3,2,1,0:T(8,128)S(1)}, u32[]{:S(2)}, u32[]{:S(2)}) collective-permute-start(f32[2,2,2,8,128]{4,3,2,1,0:T(8,128)S(1)} %fusion.4.refs_4_), channel_id=1, source_target_pairs={{0,0},{8,32},{16,64},{24,96},{32,8},{40,40},{48,72},{56,104},{64,1... | collective-permute-start | bytes 98312 | tf_op jit(solution)/shard_map/ppermute | solution.py:251
  278.8 5.0 %collective-permute-start.50 = (f32[2,2,2,8,128]{4,3,2,1,0:T(8,128)S(1)}, f32[2,2,2,8,128]{4,3,2,1,0:T(8,128)S(1)}, u32[]{:S(2)}, u32[]{:S(2)}) collective-permute-start(f32[2,2,2,8,128]{4,3,2,1,0:T(8,128)S(1)} %fusion.4.refs_4_), channel_id=1, source_target_pairs={{0,96},{8,0},{16,32},{24,64},{32,104},{40,8},{48,40},{56,72},{64,1... | collective-permute-start | bytes 98312 | tf_op jit(solution)/shard_map/ppermute | solution.py:251
  282.7 4.6 %collective-permute-start.49 = (f32[2,2,2,8,128]{4,3,2,1,0:T(8,128)S(1)}, f32[2,2,2,8,128]{4,3,2,1,0:T(8,128)S(1)}, u32[]{:S(2)}, u32[]{:S(2)}) collective-permute-start(f32[2,2,2,8,128]{4,3,2,1,0:T(8,128)S(1)} %fusion.4.refs_4_), channel_id=1, source_target_pairs={{0,64},{8,96},{16,0},{24,32},{32,72},{40,104},{48,8},{56,40},{64,8... | collective-permute-start | bytes 98312 | tf_op jit(solution)/shard_map/ppermute | solution.py:251
  282.8 25.5 %collective-permute-start.46 = (f32[8,2,2,8,128]{4,3,2,1,0:T(8,128)S(1)}, f32[8,2,2,8,128]{4,3,2,1,0:T(8,128)S(1)}, u32[]{:S(2)}, u32[]{:S(2)}) collective-permute-start(f32[8,2,2,8,128]{4,3,2,1,0:T(8,128)S(1)} %pad_maximum_fusion.1), channel_id=1, source_target_pairs={{0,32},{8,40},{16,48},{24,56},{32,64},{40,72},{48,80},{56,88},{64,... | collective-permute-start | bytes 393224 | tf_op jit(solution)/shard_map/ppermute | solution.py:251
  282.9 25.4 %collective-permute-start.45 = (f32[8,2,2,8,128]{4,3,2,1,0:T(8,128)S(1)}, f32[8,2,2,8,128]{4,3,2,1,0:T(8,128)S(1)}, u32[]{:S(2)}, u32[]{:S(2)}) collective-permute-start(f32[8,2,2,8,128]{4,3,2,1,0:T(8,128)S(1)} %pad_maximum_fusion.1), channel_id=1, source_target_pairs={{0,64},{8,72},{16,80},{24,88},{32,96},{40,104},{48,112},{56,120},{... | collective-permute-start | bytes 393224 | tf_op jit(solution)/shard_map/ppermute | solution.py:251
  283.5 24.9 %collective-permute-start.44 = (f32[8,2,2,8,128]{4,3,2,1,0:T(8,128)S(1)}, f32[8,2,2,8,128]{4,3,2,1,0:T(8,128)S(1)}, u32[]{:S(2)}, u32[]{:S(2)}) collective-permute-start(f32[8,2,2,8,128]{4,3,2,1,0:T(8,128)S(1)} %pad_maximum_fusion.1), channel_id=1, source_target_pairs={{0,96},{8,104},{16,112},{24,120},{32,0},{40,8},{48,16},{56,24},{64... | collective-permute-start | bytes 393224 | tf_op jit(solution)/shard_map/ppermute | solution.py:251

commit v2 on v1

v2 whole, which is shorter than its diff:
```python
import functools

import jax
import jax.numpy as jnp
import numpy as np
from jax import lax
from jax.experimental import pallas as pl
from jax.experimental.pallas import tpu as pltpu
from jax.sharding import PartitionSpec as P

ITERS = 3
GRID = ("row", "col")
VMEM_LIMIT = 60 * 1024 * 1024
TILE = 16


def spread_matrix(count):
    spread = np.zeros((count, 2, 2, count, 2, TILE), np.float32)
    for k in range(count):
        spread[k, 0, 0, k, 0] = 1.0
        spread[k, 1, 0, k, 1] = -1.0
        spread[k, 1, 1, k, 0] = 1.0
        spread[k, 0, 1, k, 1] = 1.0
    return spread.reshape(2 * count, 4 * count * TILE)


def split(value):
    high = value.astype(jnp.bfloat16)
    low = (value - high.astype(jnp.float32)).astype(jnp.bfloat16)
    return high, low


def kernel(first, precise, final, place, *refs):
    refs = list(refs)
    take = refs.pop
    model, vis, flags, spread = take(0), take(0), take(0), take(0)
    if first:
        row_in, col_in = take(0), take(0)
    else:
        gains_in = take(0)
    if final:
        resid, gains_out = take(0), take(0)
    else:
        sums_out = take(0)
    g_row, g_col, g_mat, w_row, w_col, left, masked, raw = refs
    count = model.shape[0]
    channel = pl.program_id(0)
    me_row, me_col = place[0], place[1]
    f32, bf16 = jnp.float32, jnp.bfloat16

    @pl.when(channel == 0)
    def prepare():
        if first:
            g_row[...] = row_in[...]
            g_col[...] = col_in[...]
        else:
            for k in range(count):
                for pol in range(2):
                    for part in range(2):
                        if final:
                            g_row[k, part, pol] = gains_in[2 * k + pol, me_row, part]
                            g_col[k, part, pol] = gains_in[2 * k + pol, me_col, part]
                            for block in range(4):
                                lanes = slice(block * 128, block * 128 + 128)
                                gains_out[k, part, pol, :, lanes] = gains_in[2 * k + pol, block, part]
                        else:
                            g_row[k, part, pol] = gains_in[2 * k + pol, 0, part]
                            g_col[k, part, pol] = gains_in[2 * k + pol, 1, part]
        for k in range(count):
            for pol in range(2):
                lanes = slice(pol * 128, pol * 128 + 128)
                for part in range(2):
                    g_mat[:, 2 * k + part, lanes] = g_row[k, part, pol]
                if not final:
                    for source, weights in ((g_row, w_row), (g_col, w_col)):
                        re, im = source[k, 0, pol], source[k, 1, pol]
                        for n, value in enumerate((re, im, re * re + im * im)):
                            high = value.astype(bf16).astype(f32)
                            weights[:, k, n, lanes] = high
                            weights[:, k, 4 + n, lanes] = value - high
                        zero = jnp.zeros_like(re)
                        for n in (3, 7, 8, 9, 10, 11, 12, 13, 14, 15):
                            weights[:, k, n, lanes] = zero

    gains_c = jnp.transpose(g_mat[channel])
    high, low = split(gains_c)
    width = 2 * count * TILE
    same = (
        lax.broadcasted_iota(jnp.int32, (128, 2 * width), 0) % TILE
        == lax.broadcasted_iota(jnp.int32, (128, 2 * width), 1) % TILE
    )
    for h, value in enumerate((high, low)):
        for pol in range(2):
            wide = jnp.dot(value[pol * 128 : pol * 128 + 128], spread[...], preferred_element_type=f32)
            wide = jnp.where(same, wide, 0.0).astype(bf16)
            for part in range(2):
                left[pol, :, (2 * h + part) * TILE : (2 * h + part + 1) * TILE, :] = wide[
                    :, part * width : (part + 1) * width
                ].reshape(128 // TILE, TILE, width)

    def residual_tile(step, _):
        pol, tile = step // 8, step % 8
        rows = pl.ds(pl.multiple_of(tile * TILE, TILE), TILE)
        stacks = []
        for b in range(2):
            parts, lows = [], []
            for k in range(count):
                m_re = model[k, 0, 0, 2 * pol + b, 0, rows, :].astype(f32)
                m_im = model[k, 0, 0, 2 * pol + b, 1, rows, :].astype(f32)
                q_re = g_col[k, 0, b, pl.ds(channel, 1), :]
                q_im = g_col[k, 1, b, pl.ds(channel, 1), :]
                z_re = m_re * q_re + m_im * q_im
                z_im = m_im * q_re - m_re * q_im
                for z in (z_re, z_im):
                    if final:
                        z_high, z_low = split(z)
                        parts.append(z_high)
                        lows.append(z_low)
                    else:
                        parts.append(z.astype(bf16))
            stacks.append((jnp.concatenate(parts, 0), jnp.concatenate(lows, 0) if final else None))
        gains_t = left[pol, tile]
        guess = jnp.dot(gains_t, jnp.concatenate([s[0] for s in stacks], 1), preferred_element_type=f32)
        if final:
            guess += jnp.dot(gains_t, jnp.concatenate([s[1] for s in stacks], 1), preferred_element_type=f32)
        weight = flags[0, rows, :].astype(f32)
        out_rows = pl.ds(pl.multiple_of(step * TILE, TILE), TILE)
        for b in range(2):
            for part in range(2):
                lanes = slice(b * 128, b * 128 + 128)
                total = (
                    guess[part * TILE : (part + 1) * TILE, lanes]
                    + guess[(2 + part) * TILE : (3 + part) * TILE, lanes]
                )
                seen = vis[0, 0, 2 * pol + b, part, rows, :].astype(f32)
                value = (seen - total) * weight
                if final:
                    resid[0, 0, 2 * pol + b, part, rows, :] = value.astype(bf16)
                else:
                    masked[part, out_rows, lanes] = value
        return 0

    if final:
        lax.fori_loop(0, 16, residual_tile, 0, unroll=4)
        return

    lax.fori_loop(0, 16, residual_tile, 0, unroll=4)
    weight = flags[0].astype(f32).astype(bf16)

    def sums(k, _):
        kinds = 5 if precise else 3
        planes = [[] for _ in range(kinds)]
        for pol in range(2):
            halves = [[] for _ in range(kinds)]
            for b in range(2):
                low_re = model[k, 0, 0, 2 * pol + b, 0]
                low_im = model[k, 0, 0, 2 * pol + b, 1]
                r_re = masked[0, pol * 128 : pol * 128 + 128, b * 128 : b * 128 + 128]
                r_im = masked[1, pol * 128 : pol * 128 + 128, b * 128 : b * 128 + 128]
                m_re, m_im = low_re.astype(f32), low_im.astype(f32)
                values = (r_re * m_re + r_im * m_im, r_im * m_re - r_re * m_im)
                values = split(values[0]) + split(values[1]) if precise else tuple(v.astype(bf16) for v in values)
                values += ((low_re * low_re + low_im * low_im) * weight,)
                for half, value in zip(halves, values):
                    half.append(value)
            for plane, half in zip(planes, halves):
                plane.append(jnp.concatenate(half, 1))
        planes = [jnp.concatenate(plane, 0) for plane in planes]
        by_q, by_p = w_col[channel, k].astype(bf16), w_row[channel, k].astype(bf16)
        over_q = [
            lax.dot_general(by_q, plane, (((1,), (1,)), ((), ())), preferred_element_type=f32) for plane in planes
        ]
        over_p = [jnp.dot(by_p, plane, preferred_element_type=f32) for plane in planes]
        for side, found in enumerate((over_q, over_p)):
            if precise:
                found = (found[0] + found[1], found[2] + found[3], found[4])
            for x, value in enumerate(found):
                raw[side, channel, k, x] = value[0:4] + value[4:8]
        return 0

    lax.fori_loop(0, count, sums, 0)
    last = pl.num_programs(0) - 1

    @pl.when(channel == last)
    def finish():
        for side, gains in ((0, g_row), (1, g_col)):
            sign = 1.0 if side == 0 else -1.0
            for k in range(count):
                for pol in range(2):
                    lanes = slice(pol * 128, pol * 128 + 128)
                    take_row = lambda x, n: raw[side, :, k, x, n, lanes]
                    denom = take_row(2, 2)
                    factor = 2.0 * denom + 0.25 if side == 0 else 2.0 * denom
                    top_re = take_row(0, 0) - sign * take_row(1, 1)
                    top_im = take_row(0, 1) + sign * take_row(1, 0)
                    sums_out[2 * k + pol, side, 0] = top_re + gains[k, 0, pol] * factor
                    sums_out[2 * k + pol, side, 1] = top_im + gains[k, 1, pol] * factor
                    sums_out[2 * k + pol, side, 2] = denom


def final_kernel(place, model, vis, flags, gains_in, resid, gains_out, p_rows, p_cols, q_rows):
    count = model.shape[0]
    channel = pl.program_id(0)
    me_row, me_col = place[0], place[1]
    f32, bf16 = jnp.float32, jnp.bfloat16

    @pl.when(channel == 0)
    def prepare():
        p_rows[...] = jnp.zeros_like(p_rows)
        for k in range(count):
            for pol in range(2):
                for part in range(2):
                    for block in range(4):
                        lanes = slice(block * 128, block * 128 + 128)
                        gains_out[k, part, pol, :, lanes] = gains_in[2 * k + pol, block, part]
                    p_rows[:, 2 * k + part, pol * 128 : pol * 128 + 128] = gains_in[2 * k + pol, me_row, part]
                re, im = gains_in[2 * k + pol, me_col, 0], gains_in[2 * k + pol, me_col, 1]
                for n, value in enumerate((im, re - im, re + im)):
                    q_rows[k, n, pol] = value

    p_cols[...] = jnp.transpose(p_rows[channel])

    def tile_work(step, _):
        pol, tile = step // 8, step % 8
        rows = pl.ds(pl.multiple_of(tile * TILE, TILE), TILE)
        p_tile = p_cols[pl.ds(pl.multiple_of(step * TILE, TILE), TILE), :]
        totals = [[0.0, 0.0] for _ in range(2)]
        for k in range(count):
            p_re, p_im = [jnp.broadcast_to(p_tile[:, 2 * k + n : 2 * k + n + 1], (TILE, 128)) for n in range(2)]
            for b in range(2):
                q = [q_rows[k, n, b, pl.ds(channel, 1), :] for n in range(3)]
                m_re = model[k, 0, 0, 2 * pol + b, 0, rows, :].astype(f32)
                m_im = model[k, 0, 0, 2 * pol + b, 1, rows, :].astype(f32)
                shared = q[0] * (m_re - m_im)
                z_re = m_re * q[2] - shared
                z_im = m_im * q[1] - shared
                totals[b][0] += p_re * z_re - p_im * z_im
                totals[b][1] += p_re * z_im + p_im * z_re
        weight = flags[0, rows, :].astype(f32)
        for b in range(2):
            for part in range(2):
                seen = vis[0, 0, 2 * pol + b, part, rows, :].astype(f32)
                resid[0, 0, 2 * pol + b, part, rows, :] = ((seen - totals[b][part]) * weight).astype(bf16)
        return 0

    lax.fori_loop(0, 16, tile_work, 0, unroll=2)


def finish(place, model, vis, flags, gains):
    count, channels = model.shape[0], model.shape[1]
    f32 = jnp.float32

    def whole(shape):
        return pl.BlockSpec(shape, lambda c, place: (0,) * len(shape))

    out_gains = (count, 2, 2, channels, 512)
    seen = pl.BlockSpec((1, 1, 4, 2, 128, 128), lambda c, place: (c, 0, 0, 0, 0, 0))
    return pl.pallas_call(
        final_kernel,
        out_shape=[jax.ShapeDtypeStruct(vis.shape, vis.dtype), jax.ShapeDtypeStruct(out_gains, f32)],
        grid_spec=pltpu.PrefetchScalarGridSpec(
            num_scalar_prefetch=1,
            grid=(channels,),
            in_specs=[
                pl.BlockSpec((count, 1, 1, 4, 2, 128, 128), lambda c, place: (0, c, 0, 0, 0, 0, 0)),
                seen,
                pl.BlockSpec((1, 128, 128), lambda c, place: (c, 0, 0)),
                whole(gains.shape),
            ],
            out_specs=[seen, whole(out_gains)],
            scratch_shapes=[
                pltpu.VMEM((channels, 128, 256), f32),
                pltpu.VMEM((256, 128), f32),
                pltpu.VMEM((count, 3, 2, channels, 128), f32),
            ],
        ),
        compiler_params=pltpu.CompilerParams(vmem_limit_bytes=VMEM_LIMIT),
        cost_estimate=pl.CostEstimate(flops=10**9, bytes_accessed=20 * 10**6, transcendentals=0),
    )(place, model, vis, flags, gains)


def sweep(first, precise, final, place, model, vis, flags, gains):
    count, channels = model.shape[0], model.shape[1]
    f32, bf16 = jnp.float32, jnp.bfloat16
    spread = jnp.asarray(spread_matrix(count), bf16)

    def whole(shape):
        return pl.BlockSpec(shape, lambda c, place: (0,) * len(shape))

    in_specs = [
        pl.BlockSpec((count, 1, 1, 4, 2, 128, 128), lambda c, place: (0, c, 0, 0, 0, 0, 0)),
        pl.BlockSpec((1, 1, 4, 2, 128, 128), lambda c, place: (c, 0, 0, 0, 0, 0)),
        pl.BlockSpec((1, 128, 128), lambda c, place: (c, 0, 0)),
        whole(spread.shape),
    ]
    if first:
        block = (count, 2, 2, channels, 128)
        in_specs += [
            pl.BlockSpec(block, lambda c, place: (0, 0, 0, 0, place[0])),
            pl.BlockSpec(block, lambda c, place: (0, 0, 0, 0, place[1])),
        ]
    else:
        in_specs += [whole(gains.shape)]
    if final:
        out_gains = (count, 2, 2, channels, 512)
        out_shape = [jax.ShapeDtypeStruct(vis.shape, bf16), jax.ShapeDtypeStruct(out_gains, f32)]
        out_specs = [pl.BlockSpec((1, 1, 4, 2, 128, 128), lambda c, place: (c, 0, 0, 0, 0, 0)), whole(out_gains)]
    else:
        shape = (2 * count, 2, 3, channels, 128)
        out_shape = jax.ShapeDtypeStruct(shape, f32)
        out_specs = whole(shape)
    return pl.pallas_call(
        functools.partial(kernel, first, precise, final),
        out_shape=out_shape,
        grid_spec=pltpu.PrefetchScalarGridSpec(
            num_scalar_prefetch=1,
            grid=(channels,),
            in_specs=in_specs,
            out_specs=out_specs,
            scratch_shapes=[
                pltpu.VMEM((count, 2, 2, channels, 128), f32),
                pltpu.VMEM((count, 2, 2, channels, 128), f32),
                pltpu.VMEM((channels, 2 * count, 256), f32),
                pltpu.VMEM((channels, count, 16, 256), f32),
                pltpu.VMEM((channels, count, 16, 256), f32),
                pltpu.VMEM((2, 8, 4 * TILE, 2 * count * TILE), bf16),
                pltpu.VMEM((2, 256, 256), f32),
                pltpu.VMEM((2, channels, count, 3, 4, 256), f32),
            ],
        ),
        compiler_params=pltpu.CompilerParams(vmem_limit_bytes=VMEM_LIMIT),
        cost_estimate=pl.CostEstimate(flops=10**10, bytes_accessed=20 * 10**6, transcendentals=0),
    )(place, model, vis, flags, spread, *((gains, gains) if first else (gains,)))


def smooth_kernel(everything, chan, weights, averaged, low, high, out):
    channels = averaged.shape[2]
    span = weights.shape[0]
    reach = span // 2
    index = chan[0] + lax.broadcasted_iota(jnp.int32, (channels, 128), 0)
    coverage = jnp.zeros((channels, 128), jnp.float32)
    for offset in range(span):
        source = index + (offset - reach)
        inside = ((source >= 0) & (source < chan[1])).astype(jnp.float32)
        coverage = coverage + weights[offset] * inside
    for block in range(4):
        for part in range(2):
            padded = jnp.concatenate([low[block, part], averaged[block, part], high[block, part]], 0)
            total = weights[0] * padded[0:channels]
            for offset in range(1, span):
                total = total + weights[offset] * padded[offset : offset + channels]
            value = total / coverage
            for target in range(16):
                if everything:
                    out[target, block, part] = value
                else:
                    if target // 4 == block:
                        out[target, 0, part] = value
                    if target % 4 == block:
                        out[target, 1, part] = value


def smooth(everything, averaged, kernel_weights, first, total_channels):
    reach = kernel_weights.shape[0] // 2
    channels = averaged.shape[2]
    chans = lax.axis_size("chan")
    low = lax.ppermute(averaged[:, :, channels - reach :], "chan", [(i, i + 1) for i in range(chans - 1)])
    high = lax.ppermute(averaged[:, :, :reach], "chan", [(i + 1, i) for i in range(chans - 1)])
    chan = jnp.stack([first, jnp.int32(total_channels)]).astype(jnp.int32)
    scalars = pl.BlockSpec(memory_space=pltpu.SMEM)
    blocks = pl.BlockSpec(memory_space=pltpu.VMEM)
    return pl.pallas_call(
        functools.partial(smooth_kernel, everything),
        out_shape=jax.ShapeDtypeStruct((16, 4 if everything else 2, *averaged.shape[1:]), jnp.float32),
        in_specs=[scalars, scalars, blocks, blocks, blocks],
        out_specs=blocks,
    )(chan, kernel_weights, averaged, low, high)


def local(visibilities, model, flags, gains, kernel_weights):
    channels = visibilities.shape[0]
    place = jnp.stack([lax.axis_index("row"), lax.axis_index("col")]).astype(jnp.int32)
    first = lax.axis_index("chan") * channels
    total_channels = channels * lax.axis_size("chan")
    for step in range(ITERS):
        sums = sweep(step == 0, step == ITERS - 1, False, place, model, visibilities, flags, gains)
        parts = lax.all_to_all(sums, GRID, 0, 0)
        parts = parts.reshape(4, 4, *parts.shape[1:])
        total = parts[:, :, 0].sum(1) + parts[:, :, 1].sum(0)
        averaged = 0.5 * total[:, :2] / (total[:, 2:] + 1.0)
        mine = smooth(step == ITERS - 1, averaged, kernel_weights, first, total_channels)
        gains = lax.all_to_all(mine, GRID, 0, 0)
    residual, gains_out = finish(place, model, visibilities, flags, gains)
    return gains_out, residual


def solution(mesh):
    placed = (
        P("chan", None, None, None, "row", "col"),
        P(None, "chan", None, None, None, "row", "col"),
        P("chan", "row", "col"),
        P(None, None, None, "chan", None),
        P(),
    )
    return jax.shard_map(
        local,
        mesh=mesh,
        in_specs=placed,
        out_specs=(P(None, None, None, "chan", None), P("chan", None, None, None, "row", "col")),
        check_vma=False,
    )
```

time: 314 us -> 266 us (0.85)
  starting transfers between devices: 99.7 us -> 27.3 us
  blocking collectives: 0 us -> 68.8 us
  Pallas kernels: 164 us -> 145 us
  other arithmetic: 14.1 us -> 1.32 us
  waiting for transfers between devices: 25.3 us -> 18.8 us
  local copies, waits for them, and re-layouts: 5.08 us -> 1.86 us
    ppermute x51 -> x6, starting transfers between devices: 99.7 us -> 20.3 us  [the longest x3 10.6 us: smooth(): lax.ppermute(averaged[:, :, :reach], 'chan', [(i + 1, i) for i in range(c...]
    all_to_all x0 -> x5, blocking collectives: none -> 68.8 us  [the longest x3 43.3 us: local(): gains = lax.all_to_all(mine, GRID, 0, 0)]
    pallas_call x4 -> x7, Pallas kernels: 164 us -> 145 us  [the longest x3 124 us: sweep(): pl.pallas_call(functools.partial(kernel, first, precise, final), out_shap...]
    ppermute x51 -> x6, waiting for transfers between devices: 25.3 us -> 9.95 us  [the longest x3 9.95 us: smooth(): lax.ppermute(averaged[:, :, channels - reach:], 'chan', [(i, i + 1) for i...]
    div x3 -> x0, other arithmetic: 9.73 us -> none  [smooth(): return total / coverage[:, None]]
    all_to_all x0 -> x1, waiting for transfers between devices: none -> 8.89 us  [local(): parts = lax.all_to_all(sums, GRID, 0, 0)]
    all_to_all x0 -> x1, starting transfers between devices: none -> 6.92 us  [local(): parts = lax.all_to_all(sums, GRID, 0, 0)]
    add x4 -> x3, other arithmetic: 3.27 us -> 0.03 us  [local(): total = parts[:, :, 0].sum(1) + parts[:, :, 1].sum(0)]
  transfers between devices with their start and end apart: 51 -> 7, of which waited for: 14 -> 4; matrix products, arithmetic and copies ran while one was open for 1% -> 0% of each run, Pallas kernels for 7% -> 0%
where the time goes in v2:
time: 266 us; the launch traced here: 264 us
  Pallas kernels  145 us (55%)
  blocking collectives  68.8 us (26%)
  starting transfers between devices  27.3 us (10%)
  waiting for transfers between devices  18.8 us (7%)
    pallas_call x3, Pallas kernels, sweep(): pl.pallas_call(functools.partial(kernel, first, precise, final), out_shap...  124 us
    all_to_all x3, blocking collectives, local(): gains = lax.all_to_all(mine, GRID, 0, 0)  43.3 us
    all_to_all x2, blocking collectives, local(): parts = lax.all_to_all(sums, GRID, 0, 0)  25.5 us
    pallas_call x1, Pallas kernels, finish(): pl.pallas_call(final_kernel, out_shape=[jax.ShapeDtypeStruct(vis.shape, v...  16.8 us
    ppermute x3, starting transfers between devices, smooth(): lax.ppermute(averaged[:, :, :reach], 'chan', [(i + 1, i) for i in range(c...  10.6 us
    ppermute x3, waiting for transfers between devices, smooth(): lax.ppermute(averaged[:, :, channels - reach:], 'chan', [(i, i + 1) for i...  9.95 us
    ppermute x3, starting transfers between devices, smooth(): lax.ppermute(averaged[:, :, channels - reach:], 'chan', [(i, i + 1) for i...  9.76 us
    all_to_all x1, waiting for transfers between devices, local(): parts = lax.all_to_all(sums, GRID, 0, 0)  8.89 us
  transfers between devices with their start and end apart: 7, of which 4 were waited for; matrix products, arithmetic and copies ran while one was open for 0% of the time, Pallas kernels for 0%

profile of v2, /device:TPU:25, one launch (start us, length us, event | category | flops | bytes accessed | tf_op | source)
XLA Modules:
  0.0 264.2 jit_solution(1508616080554918672)
XLA Ops:
  0.6 0.6 pad_add_fusion.place
  1.2 38.2 %shard_map.95 = f32[16,2,3,8,128]{4,3,2,1,0:T(8,128)} custom-call(s32[2]{0:T(128)} %pad_add_fusion.place, bf16[8,8,1,4,2,128,128]{6,5,4,3,2,1,0:T(8,128)(2,1)} %model.1, bf16[8,1,4,2,128,128]{5,4,3,2,1,0:T(8,128)(2,1)} %vis.1, s32[8,128,128]{2,1,0:T(8,128)} %flags.1, bf16[16,512]{1,0:T(8,128)(2,1)} %constant.24.clone.refs_3_, f32[8,2,2,8,512]{4,3,2,1,0:T(8,128)} %refs_5_.1, ...), custom_call_target="tpu_custom_call" | custom-call | flops 10000000000 | bytes 20000000 | tf_op jit(solution)/shard_map/pallas_call | solution.py:312
  39.5 6.9 %all-to-all-start = ((f32[16,2,3,8,128]{4,3,2,1,0:T(8,128)}), f32[16,2,3,8,128]{4,3,2,1,0:T(8,128)S(1)}, u32[]{:S(2)}, u32[]{:S(2)}) async-start(f32[16,2,3,8,128]{4,3,2,1,0:T(8,128)} %shard_map.95), calls=%async_computation | async-start | bytes 786432 | tf_op jit(solution)/shard_map/all_to_all | solution.py:387
  46.4 8.9 %all-to-all-done = f32[16,2,3,8,128]{4,3,2,1,0:T(8,128)S(1)} async-done(((f32[16,2,3,8,128]{4,3,2,1,0:T(8,128)}), f32[16,2,3,8,128]{4,3,2,1,0:T(8,128)S(1)}, u32[]{:S(2)}, u32[]{:S(2)}) %all-to-all-start) | async-done | bytes 393248 | tf_op jit(solution)/shard_map/all_to_all | solution.py:387
  55.3 0.0 copy-start
  55.4 4.5 %collective-permute-start.1 = (f32[4,2,2,128]{3,2,1,0:T(2,128)S(1)}, f32[4,2,2,128]{3,2,1,0:T(2,128)S(1)}, u32[]{:S(2)}, u32[]{:S(2)}) collective-permute-start(f32[4,2,2,128]{3,2,1,0:T(2,128)S(1)} %get-tuple-element.16), channel_id=1, source_target_pairs={{1,0},{2,1},{3,2},{4,3},{5,4},{6,5},{7,6},{9,8},{10,9},{11,10},{12... | collective-permute-start | bytes 24584 | tf_op jit(solution)/shard_map/ppermute | solution.py:368
  59.9 2.2 collective-permute-start
  62.2 0.6 pad_add_fusion.1.chan
  62.8 0.0 collective-permute-done.1.high
  62.8 0.0 copy-start.5
  62.8 3.9 %collective-permute-done.low = f32[4,2,2,128]{3,2,1,0:T(2,128)S(1)} collective-permute-done((f32[4,2,2,128]{3,2,1,0:T(2,128)S(1)}, f32[4,2,2,128]{3,2,1,0:T(2,128)S(1)}, u32[]{:S(2)}, u32[]{:S(2)}) %collective-permute-start) | collective-permute-done | bytes 8224 | tf_op jit(solution)/shard_map/ppermute | solution.py:367
  66.7 0.0 copy-done
  66.7 0.0 copy-done.5
  66.7 0.0 copy-start.7
  66.7 0.6 copy-done.7
  67.3 1.6 shard_map.96
  68.9 13.6 %all_to_all.30.refs_4_ = f32[16,2,2,8,128]{4,3,2,1,0:T(8,128)} all-to-all(f32[16,2,2,8,128]{4,3,2,1,0:T(8,128)} %shard_map.96), channel_id=1, replica_groups=mesh['row'=4,'col'=4,'chan'=8] {'row','col'}, dimensions={0} | all-to-all | bytes 524288 | tf_op jit(solution)/shard_map/all_to_all | solution.py:392
  82.5 38.4 %shard_map.97 = f32[16,2,3,8,128]{4,3,2,1,0:T(8,128)} custom-call(s32[2]{0:T(128)} %pad_add_fusion.place, bf16[8,8,1,4,2,128,128]{6,5,4,3,2,1,0:T(8,128)(2,1)} %model.1, bf16[8,1,4,2,128,128]{5,4,3,2,1,0:T(8,128)(2,1)} %vis.1, s32[8,128,128]{2,1,0:T(8,128)} %flags.1, bf16[16,512]{1,0:T(8,128)(2,1)} %constant.24.clone.refs_3_, ...), custom_call_target="tpu_custom_call" | custom-call | flops 10000000000 | bytes 20000000 | tf_op jit(solution)/shard_map/pallas_call | solution.py:312
  120.9 12.8 %all_to_all.31 = f32[16,2,3,8,128]{4,3,2,1,0:T(8,128)S(1)} all-to-all(f32[16,2,3,8,128]{4,3,2,1,0:T(8,128)} %shard_map.97), channel_id=1, replica_groups=mesh['row'=4,'col'=4,'chan'=8] {'row','col'}, dimensions={0} | all-to-all | bytes 786432 | tf_op jit(solution)/shard_map/all_to_all | solution.py:387
  133.7 0.0 copy-start.2
  133.8 1.9 collective-permute-start.3
  135.7 4.9 %collective-permute-start.2 = (f32[4,2,2,128]{3,2,1,0:T(2,128)S(1)}, f32[4,2,2,128]{3,2,1,0:T(2,128)S(1)}, u32[]{:S(2)}, u32[]{:S(2)}) collective-permute-start(f32[4,2,2,128]{3,2,1,0:T(2,128)S(1)} %get-tuple-element.15), channel_id=1, source_target_pairs={{0,1},{1,2},{2,3},{3,4},{4,5},{5,6},{6,7},{8,9},{9,10},{10,11},{11... | collective-permute-start | bytes 24584 | tf_op jit(solution)/shard_map/ppermute | solution.py:367
  140.6 0.0 collective-permute-done.3.high
  140.6 0.0 copy-start.6
  140.6 1.9 collective-permute-done.2.low
  142.5 0.0 copy-done.2
  142.5 0.0 copy-done.6
  142.5 0.0 copy-start.8
  142.5 0.6 copy-done.8
  143.1 1.6 shard_map.98
  144.7 13.3 %all_to_all.32.refs_4_ = f32[16,2,2,8,128]{4,3,2,1,0:T(8,128)} all-to-all(f32[16,2,2,8,128]{4,3,2,1,0:T(8,128)} %shard_map.98), channel_id=1, replica_groups=mesh['row'=4,'col'=4,'chan'=8] {'row','col'}, dimensions={0} | all-to-all | bytes 524288 | tf_op jit(solution)/shard_map/all_to_all | solution.py:392
  158.0 47.0 %shard_map.99 = f32[16,2,3,8,128]{4,3,2,1,0:T(8,128)} custom-call(s32[2]{0:T(128)} %pad_add_fusion.place, bf16[8,8,1,4,2,128,128]{6,5,4,3,2,1,0:T(8,128)(2,1)} %model.1, bf16[8,1,4,2,128,128]{5,4,3,2,1,0:T(8,128)(2,1)} %vis.1, s32[8,128,128]{2,1,0:T(8,128)} %flags.1, bf16[16,512]{1,0:T(8,128)(2,1)} %constant.24.clone.refs_3_, ...), custom_call_target="tpu_custom_call" | custom-call | flops 10000000000 | bytes 20000000 | tf_op jit(solution)/shard_map/pallas_call | solution.py:312
  205.0 12.8 %all_to_all.33 = f32[16,2,3,8,128]{4,3,2,1,0:T(8,128)S(1)} all-to-all(f32[16,2,3,8,128]{4,3,2,1,0:T(8,128)} %shard_map.99), channel_id=1, replica_groups=mesh['row'=4,'col'=4,'chan'=8] {'row','col'}, dimensions={0} | all-to-all | bytes 786432 | tf_op jit(solution)/shard_map/all_to_all | solution.py:387
  217.9 0.0 copy-start.1
  217.9 4.1 %collective-permute-start.5 = (f32[4,2,2,128]{3,2,1,0:T(2,128)S(1)}, f32[4,2,2,128]{3,2,1,0:T(2,128)S(1)}, u32[]{:S(2)}, u32[]{:S(2)}) collective-permute-start(f32[4,2,2,128]{3,2,1,0:T(2,128)S(1)} %get-tuple-element.12), channel_id=1, source_target_pairs={{1,0},{2,1},{3,2},{4,3},{5,4},{6,5},{7,6},{9,8},{10,9},{11,10},{12... | collective-permute-start | bytes 24584 | tf_op jit(solution)/shard_map/ppermute | solution.py:368
  222.0 2.6 %collective-permute-start.4 = (f32[4,2,2,128]{3,2,1,0:T(2,128)S(1)}, f32[4,2,2,128]{3,2,1,0:T(2,128)S(1)}, u32[]{:S(2)}, u32[]{:S(2)}) collective-permute-start(f32[4,2,2,128]{3,2,1,0:T(2,128)S(1)} %get-tuple-element.13), channel_id=1, source_target_pairs={{0,1},{1,2},{2,3},{3,4},{4,5},{5,6},{6,7},{8,9},{9,10},{10,11},{11... | collective-permute-start | bytes 24584 | tf_op jit(solution)/shard_map/ppermute | solution.py:367
  224.7 0.0 collective-permute-done.5.high
  224.7 0.0 copy-start.3
  224.7 4.1 %collective-permute-done.4.low = f32[4,2,2,128]{3,2,1,0:T(2,128)S(1)} collective-permute-done((f32[4,2,2,128]{3,2,1,0:T(2,128)S(1)}, f32[4,2,2,128]{3,2,1,0:T(2,128)S(1)}, u32[]{:S(2)}, u32[]{:S(2)}) %collective-permute-start.4) | collective-permute-done | bytes 8224 | tf_op jit(solution)/shard_map/ppermute | solution.py:367
  228.8 0.0 copy-done.1
  228.9 0.0 copy-done.3
  228.9 0.0 copy-start.4
  228.9 0.6 copy-done.4
  229.5 1.7 shard_map.100
  231.1 16.3 %all_to_all.34.gains_in = f32[16,4,2,8,128]{4,3,2,1,0:T(8,128)} all-to-all(f32[16,4,2,8,128]{4,3,2,1,0:T(8,128)} %shard_map.100), channel_id=1, replica_groups=mesh['row'=4,'col'=4,'chan'=8] {'row','col'}, dimensions={0} | all-to-all | bytes 1048576 | tf_op jit(solution)/shard_map/all_to_all | solution.py:392
  247.4 16.8 %shard_map.101 = (bf16[8,1,4,2,128,128]{5,4,3,2,1,0:T(8,128)(2,1)}, f32[8,2,2,8,512]{4,3,2,1,0:T(8,128)}) custom-call(s32[2]{0:T(128)} %pad_add_fusion.place, bf16[8,8,1,4,2,128,128]{6,5,4,3,2,1,0:T(8,128)(2,1)} %model.1, bf16[8,1,4,2,128,128]{5,4,3,2,1,0:T(8,128)(2,1)} %vis.1, s32[8,128,128]{2,1,0:T(8,128)} %flags.1, f32[16,4,2,8,128]{4,3,2,1,0:T(8,128)} %all_to_all.34.gains_in), custom_call_target="tpu_custom_call" | custom-call | flops 1000000000 | bytes 20000000 | tf_op jit(solution)/shard_map/pallas_call | solution.py:258
  (15 shorter events, 0.1 us)
Async XLA Ops:
  39.5 15.8 %all-to-all-start = ((f32[16,2,3,8,128]{4,3,2,1,0:T(8,128)}), f32[16,2,3,8,128]{4,3,2,1,0:T(8,128)S(1)}, u32[]{:S(2)}, u32[]{:S(2)}) async-start(f32[16,2,3,8,128]{4,3,2,1,0:T(8,128)} %shard_map.95), calls=%async_computation | async-start | bytes 786432 | tf_op jit(solution)/shard_map/all_to_all | solution.py:387
  55.3 11.4 %copy-start = (f32[4,2,8,128]{3,2,1,0:T(8,128)}, f32[4,2,8,128]{3,2,1,0:T(8,128)S(1)}, u32[]{:S(2)}) copy-start(f32[4,2,8,128]{3,2,1,0:T(8,128)S(1)} %fusion.2.averaged) | copy-start | bytes 98308
  55.4 7.4 %collective-permute-start.1 = (f32[4,2,2,128]{3,2,1,0:T(2,128)S(1)}, f32[4,2,2,128]{3,2,1,0:T(2,128)S(1)}, u32[]{:S(2)}, u32[]{:S(2)}) collective-permute-start(f32[4,2,2,128]{3,2,1,0:T(2,128)S(1)} %get-tuple-element.16), channel_id=1, source_target_pairs={{1,0},{2,1},{3,2},{4,3},{5,4},{6,5},{7,6},{9,8},{10,9},{11,10},{12... | collective-permute-start | bytes 24584 | tf_op jit(solution)/shard_map/ppermute | solution.py:368
  59.9 6.8 %collective-permute-start = (f32[4,2,2,128]{3,2,1,0:T(2,128)S(1)}, f32[4,2,2,128]{3,2,1,0:T(2,128)S(1)}, u32[]{:S(2)}, u32[]{:S(2)}) collective-permute-start(f32[4,2,2,128]{3,2,1,0:T(2,128)S(1)} %get-tuple-element.17), channel_id=1, source_target_pairs={{0,1},{1,2},{2,3},{3,4},{4,5},{5,6},{6,7},{8,9},{9,10},{10,11},{11... | collective-permute-start | bytes 24584 | tf_op jit(solution)/shard_map/ppermute | solution.py:367
  62.8 3.9 %copy-start.5 = (f32[4,2,2,128]{3,2,1,0:T(2,128)}, f32[4,2,2,128]{3,2,1,0:T(2,128)S(1)}, u32[]{:S(2)}) copy-start(f32[4,2,2,128]{3,2,1,0:T(2,128)S(1)} %collective-permute-done.1.high) | copy-start | bytes 24580
  66.7 0.6 copy-start.7
  133.7 8.8 %copy-start.2 = (f32[4,2,8,128]{3,2,1,0:T(8,128)}, f32[4,2,8,128]{3,2,1,0:T(8,128)S(1)}, u32[]{:S(2)}) copy-start(f32[4,2,8,128]{3,2,1,0:T(8,128)S(1)} %fusion.1.averaged) | copy-start | bytes 98308
  133.8 6.8 %collective-permute-start.3 = (f32[4,2,2,128]{3,2,1,0:T(2,128)S(1)}, f32[4,2,2,128]{3,2,1,0:T(2,128)S(1)}, u32[]{:S(2)}, u32[]{:S(2)}) collective-permute-start(f32[4,2,2,128]{3,2,1,0:T(2,128)S(1)} %get-tuple-element.14), channel_id=1, source_target_pairs={{1,0},{2,1},{3,2},{4,3},{5,4},{6,5},{7,6},{9,8},{10,9},{11,10},{12... | collective-permute-start | bytes 24584 | tf_op jit(solution)/shard_map/ppermute | solution.py:368
  135.7 6.8 %collective-permute-start.2 = (f32[4,2,2,128]{3,2,1,0:T(2,128)S(1)}, f32[4,2,2,128]{3,2,1,0:T(2,128)S(1)}, u32[]{:S(2)}, u32[]{:S(2)}) collective-permute-start(f32[4,2,2,128]{3,2,1,0:T(2,128)S(1)} %get-tuple-element.15), channel_id=1, source_target_pairs={{0,1},{1,2},{2,3},{3,4},{4,5},{5,6},{6,7},{8,9},{9,10},{10,11},{11... | collective-permute-start | bytes 24584 | tf_op jit(solution)/shard_map/ppermute | solution.py:367
  140.6 1.9 copy-start.6
  142.5 0.6 copy-start.8
  217.9 11.0 %copy-start.1 = (f32[4,2,8,128]{3,2,1,0:T(8,128)}, f32[4,2,8,128]{3,2,1,0:T(8,128)S(1)}, u32[]{:S(2)}) copy-start(f32[4,2,8,128]{3,2,1,0:T(8,128)S(1)} %fusion.averaged) | copy-start | bytes 98308
  217.9 6.8 %collective-permute-start.5 = (f32[4,2,2,128]{3,2,1,0:T(2,128)S(1)}, f32[4,2,2,128]{3,2,1,0:T(2,128)S(1)}, u32[]{:S(2)}, u32[]{:S(2)}) collective-permute-start(f32[4,2,2,128]{3,2,1,0:T(2,128)S(1)} %get-tuple-element.12), channel_id=1, source_target_pairs={{1,0},{2,1},{3,2},{4,3},{5,4},{6,5},{7,6},{9,8},{10,9},{11,10},{12... | collective-permute-start | bytes 24584 | tf_op jit(solution)/shard_map/ppermute | solution.py:368
  222.0 6.8 %collective-permute-start.4 = (f32[4,2,2,128]{3,2,1,0:T(2,128)S(1)}, f32[4,2,2,128]{3,2,1,0:T(2,128)S(1)}, u32[]{:S(2)}, u32[]{:S(2)}) collective-permute-start(f32[4,2,2,128]{3,2,1,0:T(2,128)S(1)} %get-tuple-element.13), channel_id=1, source_target_pairs={{0,1},{1,2},{2,3},{3,4},{4,5},{5,6},{6,7},{8,9},{9,10},{10,11},{11... | collective-permute-start | bytes 24584 | tf_op jit(solution)/shard_map/ppermute | solution.py:367
  224.7 4.1 %copy-start.3 = (f32[4,2,2,128]{3,2,1,0:T(2,128)}, f32[4,2,2,128]{3,2,1,0:T(2,128)S(1)}, u32[]{:S(2)}) copy-start(f32[4,2,2,128]{3,2,1,0:T(2,128)S(1)} %collective-permute-done.5.high) | copy-start | bytes 24580
  228.9 0.6 copy-start.4

commit v3 on v2

--- a/solution.py
+++ b/solution.py
@@ -66,6 +66,9 @@
                         else:
                             g_row[k, part, pol] = gains_in[2 * k + pol, 0, part]
                             g_col[k, part, pol] = gains_in[2 * k + pol, 1, part]
+        if not final:
+            w_row[...] = jnp.zeros_like(w_row)
+            w_col[...] = jnp.zeros_like(w_col)
         for k in range(count):
             for pol in range(2):
                 lanes = slice(pol * 128, pol * 128 + 128)
@@ -78,9 +81,6 @@
                             high = value.astype(bf16).astype(f32)
                             weights[:, k, n, lanes] = high
                             weights[:, k, 4 + n, lanes] = value - high
-                        zero = jnp.zeros_like(re)
-                        for n in (3, 7, 8, 9, 10, 11, 12, 13, 14, 15):
-                            weights[:, k, n, lanes] = zero
 
     gains_c = jnp.transpose(g_mat[channel])
     high, low = split(gains_c)
@@ -178,7 +178,7 @@
                 raw[side, channel, k, x] = value[0:4] + value[4:8]
         return 0
 
-    lax.fori_loop(0, count, sums, 0)
+    lax.fori_loop(0, count, sums, 0, unroll=4)
     last = pl.num_programs(0) - 1
 
     @pl.when(channel == last)

time: 266 us -> 239 us (0.90)
  Pallas kernels: 145 us -> 119 us
    pallas_call x3, Pallas kernels: 124 us -> 97.2 us  [sweep(): pl.pallas_call(functools.partial(kernel, first, precise, final), out_shap...]
where the time goes in v3:
time: 239 us; the launch traced here: 238 us
  Pallas kernels  119 us (50%)
  blocking collectives  68.8 us (29%)
  starting transfers between devices  27.3 us (11%)
  waiting for transfers between devices  18.8 us (8%)
    pallas_call x3, Pallas kernels, sweep(): pl.pallas_call(functools.partial(kernel, first, precise, final), out_shap...  97.2 us
    all_to_all x3, blocking collectives, local(): gains = lax.all_to_all(mine, GRID, 0, 0)  43.3 us
    all_to_all x2, blocking collectives, local(): parts = lax.all_to_all(sums, GRID, 0, 0)  25.5 us
    pallas_call x1, Pallas kernels, finish(): pl.pallas_call(final_kernel, out_shape=[jax.ShapeDtypeStruct(vis.shape, v...  16.8 us
    ppermute x3, starting transfers between devices, smooth(): lax.ppermute(averaged[:, :, :reach], 'chan', [(i + 1, i) for i in range(c...  10.6 us
    ppermute x3, waiting for transfers between devices, smooth(): lax.ppermute(averaged[:, :, channels - reach:], 'chan', [(i, i + 1) for i...  9.95 us
    ppermute x3, starting transfers between devices, smooth(): lax.ppermute(averaged[:, :, channels - reach:], 'chan', [(i, i + 1) for i...  9.76 us
    all_to_all x1, waiting for transfers between devices, local(): parts = lax.all_to_all(sums, GRID, 0, 0)  8.89 us
  transfers between devices with their start and end apart: 7, of which 4 were waited for; matrix products, arithmetic and copies ran while one was open for 0% of the time, Pallas kernels for 0%

profile of v3, /device:TPU:25, one launch (start us, length us, event | category | flops | bytes accessed | tf_op | source)
XLA Modules:
  0.0 237.8 jit_solution(8889893362070402386)
XLA Ops:
  0.6 0.6 pad_add_fusion.place
  1.2 29.9 %shard_map.95 = f32[16,2,3,8,128]{4,3,2,1,0:T(8,128)} custom-call(s32[2]{0:T(128)} %pad_add_fusion.place, bf16[8,8,1,4,2,128,128]{6,5,4,3,2,1,0:T(8,128)(2,1)} %model.1, bf16[8,1,4,2,128,128]{5,4,3,2,1,0:T(8,128)(2,1)} %vis.1, s32[8,128,128]{2,1,0:T(8,128)} %flags.1, bf16[16,512]{1,0:T(8,128)(2,1)} %constant.24.clone.refs_3_, f32[8,2,2,8,512]{4,3,2,1,0:T(8,128)} %refs_5_.1, ...), custom_call_target="tpu_custom_call" | custom-call | flops 10000000000 | bytes 20000000 | tf_op jit(solution)/shard_map/pallas_call | solution.py:312
  31.2 6.9 %all-to-all-start = ((f32[16,2,3,8,128]{4,3,2,1,0:T(8,128)}), f32[16,2,3,8,128]{4,3,2,1,0:T(8,128)S(1)}, u32[]{:S(2)}, u32[]{:S(2)}) async-start(f32[16,2,3,8,128]{4,3,2,1,0:T(8,128)} %shard_map.95), calls=%async_computation | async-start | bytes 786432 | tf_op jit(solution)/shard_map/all_to_all | solution.py:387
  38.1 8.9 %all-to-all-done = f32[16,2,3,8,128]{4,3,2,1,0:T(8,128)S(1)} async-done(((f32[16,2,3,8,128]{4,3,2,1,0:T(8,128)}), f32[16,2,3,8,128]{4,3,2,1,0:T(8,128)S(1)}, u32[]{:S(2)}, u32[]{:S(2)}) %all-to-all-start) | async-done | bytes 393248 | tf_op jit(solution)/shard_map/all_to_all | solution.py:387
  47.1 0.0 copy-start
  47.1 4.5 %collective-permute-start.1 = (f32[4,2,2,128]{3,2,1,0:T(2,128)S(1)}, f32[4,2,2,128]{3,2,1,0:T(2,128)S(1)}, u32[]{:S(2)}, u32[]{:S(2)}) collective-permute-start(f32[4,2,2,128]{3,2,1,0:T(2,128)S(1)} %get-tuple-element.16), channel_id=1, source_target_pairs={{1,0},{2,1},{3,2},{4,3},{5,4},{6,5},{7,6},{9,8},{10,9},{11,10},{12... | collective-permute-start | bytes 24584 | tf_op jit(solution)/shard_map/ppermute | solution.py:368
  51.6 2.2 collective-permute-start
  53.9 0.6 pad_add_fusion.1.chan
  54.5 0.0 collective-permute-done.1.high
  54.5 0.0 copy-start.5
  54.5 3.9 %collective-permute-done.low = f32[4,2,2,128]{3,2,1,0:T(2,128)S(1)} collective-permute-done((f32[4,2,2,128]{3,2,1,0:T(2,128)S(1)}, f32[4,2,2,128]{3,2,1,0:T(2,128)S(1)}, u32[]{:S(2)}, u32[]{:S(2)}) %collective-permute-start) | collective-permute-done | bytes 8224 | tf_op jit(solution)/shard_map/ppermute | solution.py:367
  58.4 0.0 copy-done
  58.4 0.0 copy-done.5
  58.4 0.0 copy-start.7
  58.4 0.6 copy-done.7
  59.0 1.6 shard_map.96
  60.6 13.6 %all_to_all.30.refs_4_ = f32[16,2,2,8,128]{4,3,2,1,0:T(8,128)} all-to-all(f32[16,2,2,8,128]{4,3,2,1,0:T(8,128)} %shard_map.96), channel_id=1, replica_groups=mesh['row'=4,'col'=4,'chan'=8] {'row','col'}, dimensions={0} | all-to-all | bytes 524288 | tf_op jit(solution)/shard_map/all_to_all | solution.py:392
  74.2 29.9 %shard_map.97 = f32[16,2,3,8,128]{4,3,2,1,0:T(8,128)} custom-call(s32[2]{0:T(128)} %pad_add_fusion.place, bf16[8,8,1,4,2,128,128]{6,5,4,3,2,1,0:T(8,128)(2,1)} %model.1, bf16[8,1,4,2,128,128]{5,4,3,2,1,0:T(8,128)(2,1)} %vis.1, s32[8,128,128]{2,1,0:T(8,128)} %flags.1, bf16[16,512]{1,0:T(8,128)(2,1)} %constant.24.clone.refs_3_, ...), custom_call_target="tpu_custom_call" | custom-call | flops 10000000000 | bytes 20000000 | tf_op jit(solution)/shard_map/pallas_call | solution.py:312
  104.1 12.8 %all_to_all.31 = f32[16,2,3,8,128]{4,3,2,1,0:T(8,128)S(1)} all-to-all(f32[16,2,3,8,128]{4,3,2,1,0:T(8,128)} %shard_map.97), channel_id=1, replica_groups=mesh['row'=4,'col'=4,'chan'=8] {'row','col'}, dimensions={0} | all-to-all | bytes 786432 | tf_op jit(solution)/shard_map/all_to_all | solution.py:387
  117.0 0.0 copy-start.2
  117.0 1.9 collective-permute-start.3
  118.9 4.9 %collective-permute-start.2 = (f32[4,2,2,128]{3,2,1,0:T(2,128)S(1)}, f32[4,2,2,128]{3,2,1,0:T(2,128)S(1)}, u32[]{:S(2)}, u32[]{:S(2)}) collective-permute-start(f32[4,2,2,128]{3,2,1,0:T(2,128)S(1)} %get-tuple-element.15), channel_id=1, source_target_pairs={{0,1},{1,2},{2,3},{3,4},{4,5},{5,6},{6,7},{8,9},{9,10},{10,11},{11... | collective-permute-start | bytes 24584 | tf_op jit(solution)/shard_map/ppermute | solution.py:367
  123.8 0.0 collective-permute-done.3.high
  123.8 0.0 copy-start.6
  123.8 1.9 collective-permute-done.2.low
  125.7 0.0 copy-done.2
  125.7 0.0 copy-done.6
  125.7 0.0 copy-start.8
  125.7 0.6 copy-done.8
  126.3 1.6 shard_map.98
  127.9 13.3 %all_to_all.32.refs_4_ = f32[16,2,2,8,128]{4,3,2,1,0:T(8,128)} all-to-all(f32[16,2,2,8,128]{4,3,2,1,0:T(8,128)} %shard_map.98), channel_id=1, replica_groups=mesh['row'=4,'col'=4,'chan'=8] {'row','col'}, dimensions={0} | all-to-all | bytes 524288 | tf_op jit(solution)/shard_map/all_to_all | solution.py:392
  141.2 37.4 %shard_map.99 = f32[16,2,3,8,128]{4,3,2,1,0:T(8,128)} custom-call(s32[2]{0:T(128)} %pad_add_fusion.place, bf16[8,8,1,4,2,128,128]{6,5,4,3,2,1,0:T(8,128)(2,1)} %model.1, bf16[8,1,4,2,128,128]{5,4,3,2,1,0:T(8,128)(2,1)} %vis.1, s32[8,128,128]{2,1,0:T(8,128)} %flags.1, bf16[16,512]{1,0:T(8,128)(2,1)} %constant.24.clone.refs_3_, ...), custom_call_target="tpu_custom_call" | custom-call | flops 10000000000 | bytes 20000000 | tf_op jit(solution)/shard_map/pallas_call | solution.py:312
  178.6 12.8 %all_to_all.33 = f32[16,2,3,8,128]{4,3,2,1,0:T(8,128)S(1)} all-to-all(f32[16,2,3,8,128]{4,3,2,1,0:T(8,128)} %shard_map.99), channel_id=1, replica_groups=mesh['row'=4,'col'=4,'chan'=8] {'row','col'}, dimensions={0} | all-to-all | bytes 786432 | tf_op jit(solution)/shard_map/all_to_all | solution.py:387
  191.4 0.0 copy-start.1
  191.5 4.1 %collective-permute-start.5 = (f32[4,2,2,128]{3,2,1,0:T(2,128)S(1)}, f32[4,2,2,128]{3,2,1,0:T(2,128)S(1)}, u32[]{:S(2)}, u32[]{:S(2)}) collective-permute-start(f32[4,2,2,128]{3,2,1,0:T(2,128)S(1)} %get-tuple-element.12), channel_id=1, source_target_pairs={{1,0},{2,1},{3,2},{4,3},{5,4},{6,5},{7,6},{9,8},{10,9},{11,10},{12... | collective-permute-start | bytes 24584 | tf_op jit(solution)/shard_map/ppermute | solution.py:368
  195.6 2.6 %collective-permute-start.4 = (f32[4,2,2,128]{3,2,1,0:T(2,128)S(1)}, f32[4,2,2,128]{3,2,1,0:T(2,128)S(1)}, u32[]{:S(2)}, u32[]{:S(2)}) collective-permute-start(f32[4,2,2,128]{3,2,1,0:T(2,128)S(1)} %get-tuple-element.13), channel_id=1, source_target_pairs={{0,1},{1,2},{2,3},{3,4},{4,5},{5,6},{6,7},{8,9},{9,10},{10,11},{11... | collective-permute-start | bytes 24584 | tf_op jit(solution)/shard_map/ppermute | solution.py:367
  198.2 0.0 collective-permute-done.5.high
  198.3 0.0 copy-start.3
  198.3 4.1 %collective-permute-done.4.low = f32[4,2,2,128]{3,2,1,0:T(2,128)S(1)} collective-permute-done((f32[4,2,2,128]{3,2,1,0:T(2,128)S(1)}, f32[4,2,2,128]{3,2,1,0:T(2,128)S(1)}, u32[]{:S(2)}, u32[]{:S(2)}) %collective-permute-start.4) | collective-permute-done | bytes 8224 | tf_op jit(solution)/shard_map/ppermute | solution.py:367
  202.4 0.0 copy-done.1
  202.4 0.0 copy-done.3
  202.4 0.0 copy-start.4
  202.4 0.6 copy-done.4
  203.0 1.7 shard_map.100
  204.7 16.3 %all_to_all.34.gains_in = f32[16,4,2,8,128]{4,3,2,1,0:T(8,128)} all-to-all(f32[16,4,2,8,128]{4,3,2,1,0:T(8,128)} %shard_map.100), channel_id=1, replica_groups=mesh['row'=4,'col'=4,'chan'=8] {'row','col'}, dimensions={0} | all-to-all | bytes 1048576 | tf_op jit(solution)/shard_map/all_to_all | solution.py:392
  221.0 16.8 %shard_map.101 = (bf16[8,1,4,2,128,128]{5,4,3,2,1,0:T(8,128)(2,1)}, f32[8,2,2,8,512]{4,3,2,1,0:T(8,128)}) custom-call(s32[2]{0:T(128)} %pad_add_fusion.place, bf16[8,8,1,4,2,128,128]{6,5,4,3,2,1,0:T(8,128)(2,1)} %model.1, bf16[8,1,4,2,128,128]{5,4,3,2,1,0:T(8,128)(2,1)} %vis.1, s32[8,128,128]{2,1,0:T(8,128)} %flags.1, f32[16,4,2,8,128]{4,3,2,1,0:T(8,128)} %all_to_all.34.gains_in), custom_call_target="tpu_custom_call" | custom-call | flops 1000000000 | bytes 20000000 | tf_op jit(solution)/shard_map/pallas_call | solution.py:258
  (15 shorter events, 0.1 us)
Async XLA Ops:
  31.2 15.8 %all-to-all-start = ((f32[16,2,3,8,128]{4,3,2,1,0:T(8,128)}), f32[16,2,3,8,128]{4,3,2,1,0:T(8,128)S(1)}, u32[]{:S(2)}, u32[]{:S(2)}) async-start(f32[16,2,3,8,128]{4,3,2,1,0:T(8,128)} %shard_map.95), calls=%async_computation | async-start | bytes 786432 | tf_op jit(solution)/shard_map/all_to_all | solution.py:387
  47.1 11.4 %copy-start = (f32[4,2,8,128]{3,2,1,0:T(8,128)}, f32[4,2,8,128]{3,2,1,0:T(8,128)S(1)}, u32[]{:S(2)}) copy-start(f32[4,2,8,128]{3,2,1,0:T(8,128)S(1)} %fusion.2.averaged) | copy-start | bytes 98308
  47.1 7.4 %collective-permute-start.1 = (f32[4,2,2,128]{3,2,1,0:T(2,128)S(1)}, f32[4,2,2,128]{3,2,1,0:T(2,128)S(1)}, u32[]{:S(2)}, u32[]{:S(2)}) collective-permute-start(f32[4,2,2,128]{3,2,1,0:T(2,128)S(1)} %get-tuple-element.16), channel_id=1, source_target_pairs={{1,0},{2,1},{3,2},{4,3},{5,4},{6,5},{7,6},{9,8},{10,9},{11,10},{12... | collective-permute-start | bytes 24584 | tf_op jit(solution)/shard_map/ppermute | solution.py:368
  51.6 6.8 %collective-permute-start = (f32[4,2,2,128]{3,2,1,0:T(2,128)S(1)}, f32[4,2,2,128]{3,2,1,0:T(2,128)S(1)}, u32[]{:S(2)}, u32[]{:S(2)}) collective-permute-start(f32[4,2,2,128]{3,2,1,0:T(2,128)S(1)} %get-tuple-element.17), channel_id=1, source_target_pairs={{0,1},{1,2},{2,3},{3,4},{4,5},{5,6},{6,7},{8,9},{9,10},{10,11},{11... | collective-permute-start | bytes 24584 | tf_op jit(solution)/shard_map/ppermute | solution.py:367
  54.5 3.9 %copy-start.5 = (f32[4,2,2,128]{3,2,1,0:T(2,128)}, f32[4,2,2,128]{3,2,1,0:T(2,128)S(1)}, u32[]{:S(2)}) copy-start(f32[4,2,2,128]{3,2,1,0:T(2,128)S(1)} %collective-permute-done.1.high) | copy-start | bytes 24580
  58.4 0.6 copy-start.7
  117.0 8.8 %copy-start.2 = (f32[4,2,8,128]{3,2,1,0:T(8,128)}, f32[4,2,8,128]{3,2,1,0:T(8,128)S(1)}, u32[]{:S(2)}) copy-start(f32[4,2,8,128]{3,2,1,0:T(8,128)S(1)} %fusion.1.averaged) | copy-start | bytes 98308
  117.0 6.8 %collective-permute-start.3 = (f32[4,2,2,128]{3,2,1,0:T(2,128)S(1)}, f32[4,2,2,128]{3,2,1,0:T(2,128)S(1)}, u32[]{:S(2)}, u32[]{:S(2)}) collective-permute-start(f32[4,2,2,128]{3,2,1,0:T(2,128)S(1)} %get-tuple-element.14), channel_id=1, source_target_pairs={{1,0},{2,1},{3,2},{4,3},{5,4},{6,5},{7,6},{9,8},{10,9},{11,10},{12... | collective-permute-start | bytes 24584 | tf_op jit(solution)/shard_map/ppermute | solution.py:368
  118.9 6.8 %collective-permute-start.2 = (f32[4,2,2,128]{3,2,1,0:T(2,128)S(1)}, f32[4,2,2,128]{3,2,1,0:T(2,128)S(1)}, u32[]{:S(2)}, u32[]{:S(2)}) collective-permute-start(f32[4,2,2,128]{3,2,1,0:T(2,128)S(1)} %get-tuple-element.15), channel_id=1, source_target_pairs={{0,1},{1,2},{2,3},{3,4},{4,5},{5,6},{6,7},{8,9},{9,10},{10,11},{11... | collective-permute-start | bytes 24584 | tf_op jit(solution)/shard_map/ppermute | solution.py:367
  123.8 1.9 copy-start.6
  125.7 0.6 copy-start.8
  191.4 11.0 %copy-start.1 = (f32[4,2,8,128]{3,2,1,0:T(8,128)}, f32[4,2,8,128]{3,2,1,0:T(8,128)S(1)}, u32[]{:S(2)}) copy-start(f32[4,2,8,128]{3,2,1,0:T(8,128)S(1)} %fusion.averaged) | copy-start | bytes 98308
  191.5 6.8 %collective-permute-start.5 = (f32[4,2,2,128]{3,2,1,0:T(2,128)S(1)}, f32[4,2,2,128]{3,2,1,0:T(2,128)S(1)}, u32[]{:S(2)}, u32[]{:S(2)}) collective-permute-start(f32[4,2,2,128]{3,2,1,0:T(2,128)S(1)} %get-tuple-element.12), channel_id=1, source_target_pairs={{1,0},{2,1},{3,2},{4,3},{5,4},{6,5},{7,6},{9,8},{10,9},{11,10},{12... | collective-permute-start | bytes 24584 | tf_op jit(solution)/shard_map/ppermute | solution.py:368
  195.6 6.8 %collective-permute-start.4 = (f32[4,2,2,128]{3,2,1,0:T(2,128)S(1)}, f32[4,2,2,128]{3,2,1,0:T(2,128)S(1)}, u32[]{:S(2)}, u32[]{:S(2)}) collective-permute-start(f32[4,2,2,128]{3,2,1,0:T(2,128)S(1)} %get-tuple-element.13), channel_id=1, source_target_pairs={{0,1},{1,2},{2,3},{3,4},{4,5},{5,6},{6,7},{8,9},{9,10},{10,11},{11... | collective-permute-start | bytes 24584 | tf_op jit(solution)/shard_map/ppermute | solution.py:367
  198.3 4.1 %copy-start.3 = (f32[4,2,2,128]{3,2,1,0:T(2,128)}, f32[4,2,2,128]{3,2,1,0:T(2,128)S(1)}, u32[]{:S(2)}) copy-start(f32[4,2,2,128]{3,2,1,0:T(2,128)S(1)} %collective-permute-done.5.high) | copy-start | bytes 24580
  202.4 0.6 copy-start.4

commit v4 on v3

--- a/solution.py
+++ b/solution.py
@@ -178,7 +178,7 @@
                 raw[side, channel, k, x] = value[0:4] + value[4:8]
         return 0
 
-    lax.fori_loop(0, count, sums, 0, unroll=4)
+    lax.fori_loop(0, count, sums, 0, unroll=8)
     last = pl.num_programs(0) - 1
 
     @pl.when(channel == last)
@@ -243,7 +243,7 @@
                 resid[0, 0, 2 * pol + b, part, rows, :] = ((seen - totals[b][part]) * weight).astype(bf16)
         return 0
 
-    lax.fori_loop(0, 16, tile_work, 0, unroll=2)
+    lax.fori_loop(0, 16, tile_work, 0, unroll=4)
 
 
 def finish(place, model, vis, flags, gains):

time: 239 us -> 235 us (0.983)
  Pallas kernels: 119 us -> 115 us
    pallas_call x3, Pallas kernels: 97.2 us -> 93.6 us  [sweep(): pl.pallas_call(functools.partial(kernel, first, precise, final), out_shap...]
where the time goes in v4:
time: 235 us; the launch traced here: 234 us
  Pallas kernels  115 us (49%)
  blocking collectives  68.8 us (29%)
  starting transfers between devices  27.3 us (12%)
  waiting for transfers between devices  18.8 us (8%)
    pallas_call x3, Pallas kernels, sweep(): pl.pallas_call(functools.partial(kernel, first, precise, final), out_shap...  93.6 us
    all_to_all x3, blocking collectives, local(): gains = lax.all_to_all(mine, GRID, 0, 0)  43.3 us
    all_to_all x2, blocking collectives, local(): parts = lax.all_to_all(sums, GRID, 0, 0)  25.5 us
    pallas_call x1, Pallas kernels, finish(): pl.pallas_call(final_kernel, out_shape=[jax.ShapeDtypeStruct(vis.shape, v...  16.2 us
    ppermute x3, starting transfers between devices, smooth(): lax.ppermute(averaged[:, :, :reach], 'chan', [(i + 1, i) for i in range(c...  10.6 us
    ppermute x3, waiting for transfers between devices, smooth(): lax.ppermute(averaged[:, :, channels - reach:], 'chan', [(i, i + 1) for i...  9.94 us
    ppermute x3, starting transfers between devices, smooth(): lax.ppermute(averaged[:, :, channels - reach:], 'chan', [(i, i + 1) for i...  9.77 us
    all_to_all x1, waiting for transfers between devices, local(): parts = lax.all_to_all(sums, GRID, 0, 0)  8.89 us
  transfers between devices with their start and end apart: 7, of which 4 were waited for; matrix products, arithmetic and copies ran while one was open for 0% of the time, Pallas kernels for 0%

profile of v4, /device:TPU:25, one launch (start us, length us, event | category | flops | bytes accessed | tf_op | source)
XLA Modules:
  0.0 233.6 jit_solution(903012590579711400)
XLA Ops:
  0.6 0.6 pad_add_fusion.place
  1.2 28.9 %shard_map.95 = f32[16,2,3,8,128]{4,3,2,1,0:T(8,128)} custom-call(s32[2]{0:T(128)} %pad_add_fusion.place, bf16[8,8,1,4,2,128,128]{6,5,4,3,2,1,0:T(8,128)(2,1)} %model.1, bf16[8,1,4,2,128,128]{5,4,3,2,1,0:T(8,128)(2,1)} %vis.1, s32[8,128,128]{2,1,0:T(8,128)} %flags.1, bf16[16,512]{1,0:T(8,128)(2,1)} %constant.24.clone.refs_3_, f32[8,2,2,8,512]{4,3,2,1,0:T(8,128)} %refs_5_.1, ...), custom_call_target="tpu_custom_call" | custom-call | flops 10000000000 | bytes 20000000 | tf_op jit(solution)/shard_map/pallas_call | solution.py:312
  30.1 6.9 %all-to-all-start = ((f32[16,2,3,8,128]{4,3,2,1,0:T(8,128)}), f32[16,2,3,8,128]{4,3,2,1,0:T(8,128)S(1)}, u32[]{:S(2)}, u32[]{:S(2)}) async-start(f32[16,2,3,8,128]{4,3,2,1,0:T(8,128)} %shard_map.95), calls=%async_computation | async-start | bytes 786432 | tf_op jit(solution)/shard_map/all_to_all | solution.py:387
  37.0 8.9 %all-to-all-done = f32[16,2,3,8,128]{4,3,2,1,0:T(8,128)S(1)} async-done(((f32[16,2,3,8,128]{4,3,2,1,0:T(8,128)}), f32[16,2,3,8,128]{4,3,2,1,0:T(8,128)S(1)}, u32[]{:S(2)}, u32[]{:S(2)}) %all-to-all-start) | async-done | bytes 393248 | tf_op jit(solution)/shard_map/all_to_all | solution.py:387
  46.0 0.0 copy-start
  46.0 4.5 %collective-permute-start.1 = (f32[4,2,2,128]{3,2,1,0:T(2,128)S(1)}, f32[4,2,2,128]{3,2,1,0:T(2,128)S(1)}, u32[]{:S(2)}, u32[]{:S(2)}) collective-permute-start(f32[4,2,2,128]{3,2,1,0:T(2,128)S(1)} %get-tuple-element.16), channel_id=1, source_target_pairs={{1,0},{2,1},{3,2},{4,3},{5,4},{6,5},{7,6},{9,8},{10,9},{11,10},{12... | collective-permute-start | bytes 24584 | tf_op jit(solution)/shard_map/ppermute | solution.py:368
  50.5 2.2 collective-permute-start
  52.8 0.6 pad_add_fusion.1.chan
  53.4 0.0 collective-permute-done.1.high
  53.4 0.0 copy-start.5
  53.4 3.9 %collective-permute-done.low = f32[4,2,2,128]{3,2,1,0:T(2,128)S(1)} collective-permute-done((f32[4,2,2,128]{3,2,1,0:T(2,128)S(1)}, f32[4,2,2,128]{3,2,1,0:T(2,128)S(1)}, u32[]{:S(2)}, u32[]{:S(2)}) %collective-permute-start) | collective-permute-done | bytes 8224 | tf_op jit(solution)/shard_map/ppermute | solution.py:367
  57.3 0.0 copy-done
  57.3 0.0 copy-done.5
  57.3 0.0 copy-start.7
  57.3 0.6 copy-done.7
  57.9 1.6 shard_map.96
  59.5 13.6 %all_to_all.30.refs_4_ = f32[16,2,2,8,128]{4,3,2,1,0:T(8,128)} all-to-all(f32[16,2,2,8,128]{4,3,2,1,0:T(8,128)} %shard_map.96), channel_id=1, replica_groups=mesh['row'=4,'col'=4,'chan'=8] {'row','col'}, dimensions={0} | all-to-all | bytes 524288 | tf_op jit(solution)/shard_map/all_to_all | solution.py:392
  73.1 28.8 %shard_map.97 = f32[16,2,3,8,128]{4,3,2,1,0:T(8,128)} custom-call(s32[2]{0:T(128)} %pad_add_fusion.place, bf16[8,8,1,4,2,128,128]{6,5,4,3,2,1,0:T(8,128)(2,1)} %model.1, bf16[8,1,4,2,128,128]{5,4,3,2,1,0:T(8,128)(2,1)} %vis.1, s32[8,128,128]{2,1,0:T(8,128)} %flags.1, bf16[16,512]{1,0:T(8,128)(2,1)} %constant.24.clone.refs_3_, ...), custom_call_target="tpu_custom_call" | custom-call | flops 10000000000 | bytes 20000000 | tf_op jit(solution)/shard_map/pallas_call | solution.py:312
  101.9 12.8 %all_to_all.31 = f32[16,2,3,8,128]{4,3,2,1,0:T(8,128)S(1)} all-to-all(f32[16,2,3,8,128]{4,3,2,1,0:T(8,128)} %shard_map.97), channel_id=1, replica_groups=mesh['row'=4,'col'=4,'chan'=8] {'row','col'}, dimensions={0} | all-to-all | bytes 786432 | tf_op jit(solution)/shard_map/all_to_all | solution.py:387
  114.8 0.0 copy-start.2
  114.8 1.9 collective-permute-start.3
  116.7 4.9 %collective-permute-start.2 = (f32[4,2,2,128]{3,2,1,0:T(2,128)S(1)}, f32[4,2,2,128]{3,2,1,0:T(2,128)S(1)}, u32[]{:S(2)}, u32[]{:S(2)}) collective-permute-start(f32[4,2,2,128]{3,2,1,0:T(2,128)S(1)} %get-tuple-element.15), channel_id=1, source_target_pairs={{0,1},{1,2},{2,3},{3,4},{4,5},{5,6},{6,7},{8,9},{9,10},{10,11},{11... | collective-permute-start | bytes 24584 | tf_op jit(solution)/shard_map/ppermute | solution.py:367
  121.6 0.0 collective-permute-done.3.high
  121.6 0.0 copy-start.6
  121.6 1.9 collective-permute-done.2.low
  123.5 0.0 copy-done.2
  123.5 0.0 copy-done.6
  123.5 0.0 copy-start.8
  123.5 0.6 copy-done.8
  124.1 1.6 shard_map.98
  125.7 13.3 %all_to_all.32.refs_4_ = f32[16,2,2,8,128]{4,3,2,1,0:T(8,128)} all-to-all(f32[16,2,2,8,128]{4,3,2,1,0:T(8,128)} %shard_map.98), channel_id=1, replica_groups=mesh['row'=4,'col'=4,'chan'=8] {'row','col'}, dimensions={0} | all-to-all | bytes 524288 | tf_op jit(solution)/shard_map/all_to_all | solution.py:392
  139.0 35.9 %shard_map.99 = f32[16,2,3,8,128]{4,3,2,1,0:T(8,128)} custom-call(s32[2]{0:T(128)} %pad_add_fusion.place, bf16[8,8,1,4,2,128,128]{6,5,4,3,2,1,0:T(8,128)(2,1)} %model.1, bf16[8,1,4,2,128,128]{5,4,3,2,1,0:T(8,128)(2,1)} %vis.1, s32[8,128,128]{2,1,0:T(8,128)} %flags.1, bf16[16,512]{1,0:T(8,128)(2,1)} %constant.24.clone.refs_3_, ...), custom_call_target="tpu_custom_call" | custom-call | flops 10000000000 | bytes 20000000 | tf_op jit(solution)/shard_map/pallas_call | solution.py:312
  175.0 12.8 %all_to_all.33 = f32[16,2,3,8,128]{4,3,2,1,0:T(8,128)S(1)} all-to-all(f32[16,2,3,8,128]{4,3,2,1,0:T(8,128)} %shard_map.99), channel_id=1, replica_groups=mesh['row'=4,'col'=4,'chan'=8] {'row','col'}, dimensions={0} | all-to-all | bytes 786432 | tf_op jit(solution)/shard_map/all_to_all | solution.py:387
  187.8 0.0 copy-start.1
  187.8 4.1 %collective-permute-start.5 = (f32[4,2,2,128]{3,2,1,0:T(2,128)S(1)}, f32[4,2,2,128]{3,2,1,0:T(2,128)S(1)}, u32[]{:S(2)}, u32[]{:S(2)}) collective-permute-start(f32[4,2,2,128]{3,2,1,0:T(2,128)S(1)} %get-tuple-element.12), channel_id=1, source_target_pairs={{1,0},{2,1},{3,2},{4,3},{5,4},{6,5},{7,6},{9,8},{10,9},{11,10},{12... | collective-permute-start | bytes 24584 | tf_op jit(solution)/shard_map/ppermute | solution.py:368
  192.0 2.7 %collective-permute-start.4 = (f32[4,2,2,128]{3,2,1,0:T(2,128)S(1)}, f32[4,2,2,128]{3,2,1,0:T(2,128)S(1)}, u32[]{:S(2)}, u32[]{:S(2)}) collective-permute-start(f32[4,2,2,128]{3,2,1,0:T(2,128)S(1)} %get-tuple-element.13), channel_id=1, source_target_pairs={{0,1},{1,2},{2,3},{3,4},{4,5},{5,6},{6,7},{8,9},{9,10},{10,11},{11... | collective-permute-start | bytes 24584 | tf_op jit(solution)/shard_map/ppermute | solution.py:367
  194.6 0.0 collective-permute-done.5.high
  194.6 0.0 copy-start.3
  194.6 4.1 %collective-permute-done.4.low = f32[4,2,2,128]{3,2,1,0:T(2,128)S(1)} collective-permute-done((f32[4,2,2,128]{3,2,1,0:T(2,128)S(1)}, f32[4,2,2,128]{3,2,1,0:T(2,128)S(1)}, u32[]{:S(2)}, u32[]{:S(2)}) %collective-permute-start.4) | collective-permute-done | bytes 8224 | tf_op jit(solution)/shard_map/ppermute | solution.py:367
  198.8 0.0 copy-done.1
  198.8 0.0 copy-done.3
  198.8 0.0 copy-start.4
  198.8 0.6 copy-done.4
  199.4 1.7 shard_map.100
  201.0 16.3 %all_to_all.34.gains_in = f32[16,4,2,8,128]{4,3,2,1,0:T(8,128)} all-to-all(f32[16,4,2,8,128]{4,3,2,1,0:T(8,128)} %shard_map.100), channel_id=1, replica_groups=mesh['row'=4,'col'=4,'chan'=8] {'row','col'}, dimensions={0} | all-to-all | bytes 1048576 | tf_op jit(solution)/shard_map/all_to_all | solution.py:392
  217.3 16.2 %shard_map.101 = (bf16[8,1,4,2,128,128]{5,4,3,2,1,0:T(8,128)(2,1)}, f32[8,2,2,8,512]{4,3,2,1,0:T(8,128)}) custom-call(s32[2]{0:T(128)} %pad_add_fusion.place, bf16[8,8,1,4,2,128,128]{6,5,4,3,2,1,0:T(8,128)(2,1)} %model.1, bf16[8,1,4,2,128,128]{5,4,3,2,1,0:T(8,128)(2,1)} %vis.1, s32[8,128,128]{2,1,0:T(8,128)} %flags.1, f32[16,4,2,8,128]{4,3,2,1,0:T(8,128)} %all_to_all.34.gains_in), custom_call_target="tpu_custom_call" | custom-call | flops 1000000000 | bytes 20000000 | tf_op jit(solution)/shard_map/pallas_call | solution.py:258
  (15 shorter events, 0.1 us)
Async XLA Ops:
  30.1 15.8 %all-to-all-start = ((f32[16,2,3,8,128]{4,3,2,1,0:T(8,128)}), f32[16,2,3,8,128]{4,3,2,1,0:T(8,128)S(1)}, u32[]{:S(2)}, u32[]{:S(2)}) async-start(f32[16,2,3,8,128]{4,3,2,1,0:T(8,128)} %shard_map.95), calls=%async_computation | async-start | bytes 786432 | tf_op jit(solution)/shard_map/all_to_all | solution.py:387
  46.0 11.4 %copy-start = (f32[4,2,8,128]{3,2,1,0:T(8,128)}, f32[4,2,8,128]{3,2,1,0:T(8,128)S(1)}, u32[]{:S(2)}) copy-start(f32[4,2,8,128]{3,2,1,0:T(8,128)S(1)} %fusion.2.averaged) | copy-start | bytes 98308
  46.0 7.4 %collective-permute-start.1 = (f32[4,2,2,128]{3,2,1,0:T(2,128)S(1)}, f32[4,2,2,128]{3,2,1,0:T(2,128)S(1)}, u32[]{:S(2)}, u32[]{:S(2)}) collective-permute-start(f32[4,2,2,128]{3,2,1,0:T(2,128)S(1)} %get-tuple-element.16), channel_id=1, source_target_pairs={{1,0},{2,1},{3,2},{4,3},{5,4},{6,5},{7,6},{9,8},{10,9},{11,10},{12... | collective-permute-start | bytes 24584 | tf_op jit(solution)/shard_map/ppermute | solution.py:368
  50.5 6.8 %collective-permute-start = (f32[4,2,2,128]{3,2,1,0:T(2,128)S(1)}, f32[4,2,2,128]{3,2,1,0:T(2,128)S(1)}, u32[]{:S(2)}, u32[]{:S(2)}) collective-permute-start(f32[4,2,2,128]{3,2,1,0:T(2,128)S(1)} %get-tuple-element.17), channel_id=1, source_target_pairs={{0,1},{1,2},{2,3},{3,4},{4,5},{5,6},{6,7},{8,9},{9,10},{10,11},{11... | collective-permute-start | bytes 24584 | tf_op jit(solution)/shard_map/ppermute | solution.py:367
  53.4 3.9 %copy-start.5 = (f32[4,2,2,128]{3,2,1,0:T(2,128)}, f32[4,2,2,128]{3,2,1,0:T(2,128)S(1)}, u32[]{:S(2)}) copy-start(f32[4,2,2,128]{3,2,1,0:T(2,128)S(1)} %collective-permute-done.1.high) | copy-start | bytes 24580
  57.3 0.6 copy-start.7
  114.8 8.8 %copy-start.2 = (f32[4,2,8,128]{3,2,1,0:T(8,128)}, f32[4,2,8,128]{3,2,1,0:T(8,128)S(1)}, u32[]{:S(2)}) copy-start(f32[4,2,8,128]{3,2,1,0:T(8,128)S(1)} %fusion.1.averaged) | copy-start | bytes 98308
  114.8 6.8 %collective-permute-start.3 = (f32[4,2,2,128]{3,2,1,0:T(2,128)S(1)}, f32[4,2,2,128]{3,2,1,0:T(2,128)S(1)}, u32[]{:S(2)}, u32[]{:S(2)}) collective-permute-start(f32[4,2,2,128]{3,2,1,0:T(2,128)S(1)} %get-tuple-element.14), channel_id=1, source_target_pairs={{1,0},{2,1},{3,2},{4,3},{5,4},{6,5},{7,6},{9,8},{10,9},{11,10},{12... | collective-permute-start | bytes 24584 | tf_op jit(solution)/shard_map/ppermute | solution.py:368
  116.7 6.8 %collective-permute-start.2 = (f32[4,2,2,128]{3,2,1,0:T(2,128)S(1)}, f32[4,2,2,128]{3,2,1,0:T(2,128)S(1)}, u32[]{:S(2)}, u32[]{:S(2)}) collective-permute-start(f32[4,2,2,128]{3,2,1,0:T(2,128)S(1)} %get-tuple-element.15), channel_id=1, source_target_pairs={{0,1},{1,2},{2,3},{3,4},{4,5},{5,6},{6,7},{8,9},{9,10},{10,11},{11... | collective-permute-start | bytes 24584 | tf_op jit(solution)/shard_map/ppermute | solution.py:367
  121.6 1.9 copy-start.6
  123.5 0.6 copy-start.8
  187.8 11.0 %copy-start.1 = (f32[4,2,8,128]{3,2,1,0:T(8,128)}, f32[4,2,8,128]{3,2,1,0:T(8,128)S(1)}, u32[]{:S(2)}) copy-start(f32[4,2,8,128]{3,2,1,0:T(8,128)S(1)} %fusion.averaged) | copy-start | bytes 98308
  187.8 6.8 %collective-permute-start.5 = (f32[4,2,2,128]{3,2,1,0:T(2,128)S(1)}, f32[4,2,2,128]{3,2,1,0:T(2,128)S(1)}, u32[]{:S(2)}, u32[]{:S(2)}) collective-permute-start(f32[4,2,2,128]{3,2,1,0:T(2,128)S(1)} %get-tuple-element.12), channel_id=1, source_target_pairs={{1,0},{2,1},{3,2},{4,3},{5,4},{6,5},{7,6},{9,8},{10,9},{11,10},{12... | collective-permute-start | bytes 24584 | tf_op jit(solution)/shard_map/ppermute | solution.py:368
  192.0 6.8 %collective-permute-start.4 = (f32[4,2,2,128]{3,2,1,0:T(2,128)S(1)}, f32[4,2,2,128]{3,2,1,0:T(2,128)S(1)}, u32[]{:S(2)}, u32[]{:S(2)}) collective-permute-start(f32[4,2,2,128]{3,2,1,0:T(2,128)S(1)} %get-tuple-element.13), channel_id=1, source_target_pairs={{0,1},{1,2},{2,3},{3,4},{4,5},{5,6},{6,7},{8,9},{9,10},{10,11},{11... | collective-permute-start | bytes 24584 | tf_op jit(solution)/shard_map/ppermute | solution.py:367
  194.6 4.1 %copy-start.3 = (f32[4,2,2,128]{3,2,1,0:T(2,128)}, f32[4,2,2,128]{3,2,1,0:T(2,128)S(1)}, u32[]{:S(2)}) copy-start(f32[4,2,2,128]{3,2,1,0:T(2,128)S(1)} %collective-permute-done.5.high) | copy-start | bytes 24580
  198.8 0.6 copy-start.4

commit v5 on v4

--- a/solution.py
+++ b/solution.py
@@ -144,7 +144,7 @@
         lax.fori_loop(0, 16, residual_tile, 0, unroll=4)
         return
 
-    lax.fori_loop(0, 16, residual_tile, 0, unroll=4)
+    lax.fori_loop(0, 16, residual_tile, 0, unroll=8)
     weight = flags[0].astype(f32).astype(bf16)
 
     def sums(k, _):

time: 235 us -> 229 us (0.974)
  Pallas kernels: 115 us -> 108 us
    pallas_call x3, Pallas kernels: 93.6 us -> 87.5 us  [sweep(): pl.pallas_call(functools.partial(kernel, first, precise, final), out_shap...]
where the time goes in v5:
time: 229 us; the launch traced here: 227 us
  Pallas kernels  108 us (47%)
  blocking collectives  68.8 us (30%)
  starting transfers between devices  27.3 us (12%)
  waiting for transfers between devices  18.8 us (8%)
    pallas_call x3, Pallas kernels, sweep(): pl.pallas_call(functools.partial(kernel, first, precise, final), out_shap...  87.5 us
    all_to_all x3, blocking collectives, local(): gains = lax.all_to_all(mine, GRID, 0, 0)  43.3 us
    all_to_all x2, blocking collectives, local(): parts = lax.all_to_all(sums, GRID, 0, 0)  25.5 us
    pallas_call x1, Pallas kernels, finish(): pl.pallas_call(final_kernel, out_shape=[jax.ShapeDtypeStruct(vis.shape, v...  16.2 us
    ppermute x3, starting transfers between devices, smooth(): lax.ppermute(averaged[:, :, :reach], 'chan', [(i + 1, i) for i in range(c...  10.6 us
    ppermute x3, waiting for transfers between devices, smooth(): lax.ppermute(averaged[:, :, channels - reach:], 'chan', [(i, i + 1) for i...  9.94 us
    ppermute x3, starting transfers between devices, smooth(): lax.ppermute(averaged[:, :, channels - reach:], 'chan', [(i, i + 1) for i...  9.77 us
    all_to_all x1, waiting for transfers between devices, local(): parts = lax.all_to_all(sums, GRID, 0, 0)  8.89 us
  transfers between devices with their start and end apart: 7, of which 4 were waited for; matrix products, arithmetic and copies ran while one was open for 0% of the time, Pallas kernels for 0%

profile of v5, /device:TPU:25, one launch (start us, length us, event | category | flops | bytes accessed | tf_op | source)
XLA Modules:
  0.0 227.5 jit_solution(3105357074729420530)
XLA Ops:
  0.6 0.6 pad_add_fusion.place
  1.2 26.8 %shard_map.95 = f32[16,2,3,8,128]{4,3,2,1,0:T(8,128)} custom-call(s32[2]{0:T(128)} %pad_add_fusion.place, bf16[8,8,1,4,2,128,128]{6,5,4,3,2,1,0:T(8,128)(2,1)} %model.1, bf16[8,1,4,2,128,128]{5,4,3,2,1,0:T(8,128)(2,1)} %vis.1, s32[8,128,128]{2,1,0:T(8,128)} %flags.1, bf16[16,512]{1,0:T(8,128)(2,1)} %constant.24.clone.refs_3_, f32[8,2,2,8,512]{4,3,2,1,0:T(8,128)} %refs_5_.1, ...), custom_call_target="tpu_custom_call" | custom-call | flops 10000000000 | bytes 20000000 | tf_op jit(solution)/shard_map/pallas_call | solution.py:312
  28.0 6.9 %all-to-all-start = ((f32[16,2,3,8,128]{4,3,2,1,0:T(8,128)}), f32[16,2,3,8,128]{4,3,2,1,0:T(8,128)S(1)}, u32[]{:S(2)}, u32[]{:S(2)}) async-start(f32[16,2,3,8,128]{4,3,2,1,0:T(8,128)} %shard_map.95), calls=%async_computation | async-start | bytes 786432 | tf_op jit(solution)/shard_map/all_to_all | solution.py:387
  35.0 8.9 %all-to-all-done = f32[16,2,3,8,128]{4,3,2,1,0:T(8,128)S(1)} async-done(((f32[16,2,3,8,128]{4,3,2,1,0:T(8,128)}), f32[16,2,3,8,128]{4,3,2,1,0:T(8,128)S(1)}, u32[]{:S(2)}, u32[]{:S(2)}) %all-to-all-start) | async-done | bytes 393248 | tf_op jit(solution)/shard_map/all_to_all | solution.py:387
  43.9 0.0 copy-start
  44.0 4.5 %collective-permute-start.1 = (f32[4,2,2,128]{3,2,1,0:T(2,128)S(1)}, f32[4,2,2,128]{3,2,1,0:T(2,128)S(1)}, u32[]{:S(2)}, u32[]{:S(2)}) collective-permute-start(f32[4,2,2,128]{3,2,1,0:T(2,128)S(1)} %get-tuple-element.16), channel_id=1, source_target_pairs={{1,0},{2,1},{3,2},{4,3},{5,4},{6,5},{7,6},{9,8},{10,9},{11,10},{12... | collective-permute-start | bytes 24584 | tf_op jit(solution)/shard_map/ppermute | solution.py:368
  48.5 2.3 collective-permute-start
  50.8 0.6 pad_add_fusion.1.chan
  51.4 0.0 collective-permute-done.1.high
  51.4 0.0 copy-start.5
  51.4 3.9 %collective-permute-done.low = f32[4,2,2,128]{3,2,1,0:T(2,128)S(1)} collective-permute-done((f32[4,2,2,128]{3,2,1,0:T(2,128)S(1)}, f32[4,2,2,128]{3,2,1,0:T(2,128)S(1)}, u32[]{:S(2)}, u32[]{:S(2)}) %collective-permute-start) | collective-permute-done | bytes 8224 | tf_op jit(solution)/shard_map/ppermute | solution.py:367
  55.3 0.0 copy-done
  55.3 0.0 copy-done.5
  55.3 0.0 copy-start.7
  55.3 0.6 copy-done.7
  55.9 1.6 shard_map.96
  57.5 13.6 %all_to_all.30.refs_4_ = f32[16,2,2,8,128]{4,3,2,1,0:T(8,128)} all-to-all(f32[16,2,2,8,128]{4,3,2,1,0:T(8,128)} %shard_map.96), channel_id=1, replica_groups=mesh['row'=4,'col'=4,'chan'=8] {'row','col'}, dimensions={0} | all-to-all | bytes 524288 | tf_op jit(solution)/shard_map/all_to_all | solution.py:392
  71.1 26.8 %shard_map.97 = f32[16,2,3,8,128]{4,3,2,1,0:T(8,128)} custom-call(s32[2]{0:T(128)} %pad_add_fusion.place, bf16[8,8,1,4,2,128,128]{6,5,4,3,2,1,0:T(8,128)(2,1)} %model.1, bf16[8,1,4,2,128,128]{5,4,3,2,1,0:T(8,128)(2,1)} %vis.1, s32[8,128,128]{2,1,0:T(8,128)} %flags.1, bf16[16,512]{1,0:T(8,128)(2,1)} %constant.24.clone.refs_3_, ...), custom_call_target="tpu_custom_call" | custom-call | flops 10000000000 | bytes 20000000 | tf_op jit(solution)/shard_map/pallas_call | solution.py:312
  97.9 12.8 %all_to_all.31 = f32[16,2,3,8,128]{4,3,2,1,0:T(8,128)S(1)} all-to-all(f32[16,2,3,8,128]{4,3,2,1,0:T(8,128)} %shard_map.97), channel_id=1, replica_groups=mesh['row'=4,'col'=4,'chan'=8] {'row','col'}, dimensions={0} | all-to-all | bytes 786432 | tf_op jit(solution)/shard_map/all_to_all | solution.py:387
  110.7 0.0 copy-start.2
  110.7 1.9 collective-permute-start.3
  112.6 4.9 %collective-permute-start.2 = (f32[4,2,2,128]{3,2,1,0:T(2,128)S(1)}, f32[4,2,2,128]{3,2,1,0:T(2,128)S(1)}, u32[]{:S(2)}, u32[]{:S(2)}) collective-permute-start(f32[4,2,2,128]{3,2,1,0:T(2,128)S(1)} %get-tuple-element.15), channel_id=1, source_target_pairs={{0,1},{1,2},{2,3},{3,4},{4,5},{5,6},{6,7},{8,9},{9,10},{10,11},{11... | collective-permute-start | bytes 24584 | tf_op jit(solution)/shard_map/ppermute | solution.py:367
  117.5 0.0 collective-permute-done.3.high
  117.5 0.0 copy-start.6
  117.5 1.9 collective-permute-done.2.low
  119.4 0.0 copy-done.2
  119.4 0.0 copy-done.6
  119.4 0.0 copy-start.8
  119.4 0.6 copy-done.8
  120.0 1.6 shard_map.98
  121.6 13.3 %all_to_all.32.refs_4_ = f32[16,2,2,8,128]{4,3,2,1,0:T(8,128)} all-to-all(f32[16,2,2,8,128]{4,3,2,1,0:T(8,128)} %shard_map.98), channel_id=1, replica_groups=mesh['row'=4,'col'=4,'chan'=8] {'row','col'}, dimensions={0} | all-to-all | bytes 524288 | tf_op jit(solution)/shard_map/all_to_all | solution.py:392
  134.9 33.9 %shard_map.99 = f32[16,2,3,8,128]{4,3,2,1,0:T(8,128)} custom-call(s32[2]{0:T(128)} %pad_add_fusion.place, bf16[8,8,1,4,2,128,128]{6,5,4,3,2,1,0:T(8,128)(2,1)} %model.1, bf16[8,1,4,2,128,128]{5,4,3,2,1,0:T(8,128)(2,1)} %vis.1, s32[8,128,128]{2,1,0:T(8,128)} %flags.1, bf16[16,512]{1,0:T(8,128)(2,1)} %constant.24.clone.refs_3_, ...), custom_call_target="tpu_custom_call" | custom-call | flops 10000000000 | bytes 20000000 | tf_op jit(solution)/shard_map/pallas_call | solution.py:312
  168.9 12.8 %all_to_all.33 = f32[16,2,3,8,128]{4,3,2,1,0:T(8,128)S(1)} all-to-all(f32[16,2,3,8,128]{4,3,2,1,0:T(8,128)} %shard_map.99), channel_id=1, replica_groups=mesh['row'=4,'col'=4,'chan'=8] {'row','col'}, dimensions={0} | all-to-all | bytes 786432 | tf_op jit(solution)/shard_map/all_to_all | solution.py:387
  181.7 0.0 copy-start.1
  181.7 4.1 %collective-permute-start.5 = (f32[4,2,2,128]{3,2,1,0:T(2,128)S(1)}, f32[4,2,2,128]{3,2,1,0:T(2,128)S(1)}, u32[]{:S(2)}, u32[]{:S(2)}) collective-permute-start(f32[4,2,2,128]{3,2,1,0:T(2,128)S(1)} %get-tuple-element.12), channel_id=1, source_target_pairs={{1,0},{2,1},{3,2},{4,3},{5,4},{6,5},{7,6},{9,8},{10,9},{11,10},{12... | collective-permute-start | bytes 24584 | tf_op jit(solution)/shard_map/ppermute | solution.py:368
  185.9 2.6 %collective-permute-start.4 = (f32[4,2,2,128]{3,2,1,0:T(2,128)S(1)}, f32[4,2,2,128]{3,2,1,0:T(2,128)S(1)}, u32[]{:S(2)}, u32[]{:S(2)}) collective-permute-start(f32[4,2,2,128]{3,2,1,0:T(2,128)S(1)} %get-tuple-element.13), channel_id=1, source_target_pairs={{0,1},{1,2},{2,3},{3,4},{4,5},{5,6},{6,7},{8,9},{9,10},{10,11},{11... | collective-permute-start | bytes 24584 | tf_op jit(solution)/shard_map/ppermute | solution.py:367
  188.5 0.0 collective-permute-done.5.high
  188.5 0.0 copy-start.3
  188.5 4.1 %collective-permute-done.4.low = f32[4,2,2,128]{3,2,1,0:T(2,128)S(1)} collective-permute-done((f32[4,2,2,128]{3,2,1,0:T(2,128)S(1)}, f32[4,2,2,128]{3,2,1,0:T(2,128)S(1)}, u32[]{:S(2)}, u32[]{:S(2)}) %collective-permute-start.4) | collective-permute-done | bytes 8224 | tf_op jit(solution)/shard_map/ppermute | solution.py:367
  192.7 0.0 copy-done.1
  192.7 0.0 copy-done.3
  192.7 0.0 copy-start.4
  192.7 0.6 copy-done.4
  193.3 1.7 shard_map.100
  195.0 16.3 %all_to_all.34.gains_in = f32[16,4,2,8,128]{4,3,2,1,0:T(8,128)} all-to-all(f32[16,4,2,8,128]{4,3,2,1,0:T(8,128)} %shard_map.100), channel_id=1, replica_groups=mesh['row'=4,'col'=4,'chan'=8] {'row','col'}, dimensions={0} | all-to-all | bytes 1048576 | tf_op jit(solution)/shard_map/all_to_all | solution.py:392
  211.3 16.2 %shard_map.101 = (bf16[8,1,4,2,128,128]{5,4,3,2,1,0:T(8,128)(2,1)}, f32[8,2,2,8,512]{4,3,2,1,0:T(8,128)}) custom-call(s32[2]{0:T(128)} %pad_add_fusion.place, bf16[8,8,1,4,2,128,128]{6,5,4,3,2,1,0:T(8,128)(2,1)} %model.1, bf16[8,1,4,2,128,128]{5,4,3,2,1,0:T(8,128)(2,1)} %vis.1, s32[8,128,128]{2,1,0:T(8,128)} %flags.1, f32[16,4,2,8,128]{4,3,2,1,0:T(8,128)} %all_to_all.34.gains_in), custom_call_target="tpu_custom_call" | custom-call | flops 1000000000 | bytes 20000000 | tf_op jit(solution)/shard_map/pallas_call | solution.py:258
  (15 shorter events, 0.1 us)
Async XLA Ops:
  28.0 15.8 %all-to-all-start = ((f32[16,2,3,8,128]{4,3,2,1,0:T(8,128)}), f32[16,2,3,8,128]{4,3,2,1,0:T(8,128)S(1)}, u32[]{:S(2)}, u32[]{:S(2)}) async-start(f32[16,2,3,8,128]{4,3,2,1,0:T(8,128)} %shard_map.95), calls=%async_computation | async-start | bytes 786432 | tf_op jit(solution)/shard_map/all_to_all | solution.py:387
  43.9 11.4 %copy-start = (f32[4,2,8,128]{3,2,1,0:T(8,128)}, f32[4,2,8,128]{3,2,1,0:T(8,128)S(1)}, u32[]{:S(2)}) copy-start(f32[4,2,8,128]{3,2,1,0:T(8,128)S(1)} %fusion.2.averaged) | copy-start | bytes 98308
  44.0 7.4 %collective-permute-start.1 = (f32[4,2,2,128]{3,2,1,0:T(2,128)S(1)}, f32[4,2,2,128]{3,2,1,0:T(2,128)S(1)}, u32[]{:S(2)}, u32[]{:S(2)}) collective-permute-start(f32[4,2,2,128]{3,2,1,0:T(2,128)S(1)} %get-tuple-element.16), channel_id=1, source_target_pairs={{1,0},{2,1},{3,2},{4,3},{5,4},{6,5},{7,6},{9,8},{10,9},{11,10},{12... | collective-permute-start | bytes 24584 | tf_op jit(solution)/shard_map/ppermute | solution.py:368
  48.5 6.8 %collective-permute-start = (f32[4,2,2,128]{3,2,1,0:T(2,128)S(1)}, f32[4,2,2,128]{3,2,1,0:T(2,128)S(1)}, u32[]{:S(2)}, u32[]{:S(2)}) collective-permute-start(f32[4,2,2,128]{3,2,1,0:T(2,128)S(1)} %get-tuple-element.17), channel_id=1, source_target_pairs={{0,1},{1,2},{2,3},{3,4},{4,5},{5,6},{6,7},{8,9},{9,10},{10,11},{11... | collective-permute-start | bytes 24584 | tf_op jit(solution)/shard_map/ppermute | solution.py:367
  51.4 3.9 %copy-start.5 = (f32[4,2,2,128]{3,2,1,0:T(2,128)}, f32[4,2,2,128]{3,2,1,0:T(2,128)S(1)}, u32[]{:S(2)}) copy-start(f32[4,2,2,128]{3,2,1,0:T(2,128)S(1)} %collective-permute-done.1.high) | copy-start | bytes 24580
  55.3 0.6 copy-start.7
  110.7 8.8 %copy-start.2 = (f32[4,2,8,128]{3,2,1,0:T(8,128)}, f32[4,2,8,128]{3,2,1,0:T(8,128)S(1)}, u32[]{:S(2)}) copy-start(f32[4,2,8,128]{3,2,1,0:T(8,128)S(1)} %fusion.1.averaged) | copy-start | bytes 98308
  110.7 6.8 %collective-permute-start.3 = (f32[4,2,2,128]{3,2,1,0:T(2,128)S(1)}, f32[4,2,2,128]{3,2,1,0:T(2,128)S(1)}, u32[]{:S(2)}, u32[]{:S(2)}) collective-permute-start(f32[4,2,2,128]{3,2,1,0:T(2,128)S(1)} %get-tuple-element.14), channel_id=1, source_target_pairs={{1,0},{2,1},{3,2},{4,3},{5,4},{6,5},{7,6},{9,8},{10,9},{11,10},{12... | collective-permute-start | bytes 24584 | tf_op jit(solution)/shard_map/ppermute | solution.py:368
  112.6 6.8 %collective-permute-start.2 = (f32[4,2,2,128]{3,2,1,0:T(2,128)S(1)}, f32[4,2,2,128]{3,2,1,0:T(2,128)S(1)}, u32[]{:S(2)}, u32[]{:S(2)}) collective-permute-start(f32[4,2,2,128]{3,2,1,0:T(2,128)S(1)} %get-tuple-element.15), channel_id=1, source_target_pairs={{0,1},{1,2},{2,3},{3,4},{4,5},{5,6},{6,7},{8,9},{9,10},{10,11},{11... | collective-permute-start | bytes 24584 | tf_op jit(solution)/shard_map/ppermute | solution.py:367
  117.5 1.9 copy-start.6
  119.4 0.6 copy-start.8
  181.7 11.0 %copy-start.1 = (f32[4,2,8,128]{3,2,1,0:T(8,128)}, f32[4,2,8,128]{3,2,1,0:T(8,128)S(1)}, u32[]{:S(2)}) copy-start(f32[4,2,8,128]{3,2,1,0:T(8,128)S(1)} %fusion.averaged) | copy-start | bytes 98308
  181.7 6.8 %collective-permute-start.5 = (f32[4,2,2,128]{3,2,1,0:T(2,128)S(1)}, f32[4,2,2,128]{3,2,1,0:T(2,128)S(1)}, u32[]{:S(2)}, u32[]{:S(2)}) collective-permute-start(f32[4,2,2,128]{3,2,1,0:T(2,128)S(1)} %get-tuple-element.12), channel_id=1, source_target_pairs={{1,0},{2,1},{3,2},{4,3},{5,4},{6,5},{7,6},{9,8},{10,9},{11,10},{12... | collective-permute-start | bytes 24584 | tf_op jit(solution)/shard_map/ppermute | solution.py:368
  185.9 6.8 %collective-permute-start.4 = (f32[4,2,2,128]{3,2,1,0:T(2,128)S(1)}, f32[4,2,2,128]{3,2,1,0:T(2,128)S(1)}, u32[]{:S(2)}, u32[]{:S(2)}) collective-permute-start(f32[4,2,2,128]{3,2,1,0:T(2,128)S(1)} %get-tuple-element.13), channel_id=1, source_target_pairs={{0,1},{1,2},{2,3},{3,4},{4,5},{5,6},{6,7},{8,9},{9,10},{10,11},{11... | collective-permute-start | bytes 24584 | tf_op jit(solution)/shard_map/ppermute | solution.py:367
  188.5 4.1 %copy-start.3 = (f32[4,2,2,128]{3,2,1,0:T(2,128)}, f32[4,2,2,128]{3,2,1,0:T(2,128)S(1)}, u32[]{:S(2)}) copy-start(f32[4,2,2,128]{3,2,1,0:T(2,128)S(1)} %collective-permute-done.5.high) | copy-start | bytes 24580
  192.7 0.6 copy-start.4
